TPU v7x, 32 devices: a whole 2x2x4 slice. The times are simulated.
32 devices in a mesh: space: 8 (over y, x, core), band: 4 (over z).
Axes of the slice: x: 2, y: 2, z: 4, core: 2. Of those that a mesh axis runs over, the one named last changes fastest.
Arguments:
- blocks: float32 [2, 32, 32, 6144], P(None, 'band', 'space'), may hold values from -304 to 304
- later: float32 [256, 32, 6144], P('band', 'space'), may hold values from -304 to 304
- potential: float32 [32, 6144], P('space'), may hold values from -1.5 to 1.5
Outputs:
- h_block: float32 [2, 32, 32, 6144], P(None, 'band', 'space')
- h_later: float32 [256, 32, 6144], P('band', 'space')
All inputs are finite; a program needn't handle non-finite values.
Results may differ from a plain program's by a relative error of at most 0.00009.
Values sent between devices are 32-bit elements; how exact they have to be, the bound alone decides.
No kernel may reach another device: no remote copies, remote signals or barrier semaphores. Data moves between devices by JAX's collectives and lax.ppermute only.
A program may use at most 128 MiB of HBM per device.

v0:
```python
import functools

import jax
import jax.numpy as jnp
import numpy as np
from jax import lax
from jax.experimental import pallas as pl
from jax.experimental.pallas import tpu as pltpu
from jax.sharding import PartitionSpec as P

NZ = 96
REACH = 4
LANE = 128

stencil_weights = (-205.0 / 72.0, 8.0 / 5.0, -1.0 / 5.0, 8.0 / 315.0, -1.0 / 560.0)
half_weights = tuple(-0.5 * w for w in stencil_weights)

GROUP = 4 * NZ
HIGHEST = lax.Precision.HIGHEST


def split(x):
    high = x.astype(jnp.bfloat16)
    low = (x - high.astype(jnp.float32)).astype(jnp.bfloat16)
    return high, low


def dot(a, b, dims=((1,), (0,))):
    return lax.dot_general(a, b, (dims, ((), ())), preferred_element_type=jnp.float32)


def exact(a, b, dims=((1,), (0,))):
    return lax.dot_general(a, b, (dims, ((), ())), precision=HIGHEST, preferred_element_type=jnp.float32)


def plane_matrix(offset):
    out = np.zeros((REACH, REACH), np.float32)
    for p in range(REACH):
        for q in range(REACH):
            shift = abs(q + offset - p)
            if 1 <= shift <= REACH:
                out[p, q] = half_weights[shift]
    return out


def spread_variants(left_of_variant, count):
    eye = np.eye(count, dtype=np.float32)
    return np.stack([np.concatenate([np.kron(eye, m) for m in ms], axis=1) for ms in left_of_variant])


def z_matrix():
    a = np.arange(GROUP)[:, None]
    o = np.arange(GROUP)[None, :]
    dz = np.abs(a - o)
    same = a // NZ == o // NZ
    out = np.zeros((GROUP, GROUP), np.float64)
    for step in range(1, REACH + 1):
        out += half_weights[step] * (same & (dz == step))
    out += 3.0 * half_weights[0] * (dz == 0)
    return out.astype(np.float32)


def split_constant(x):
    high = x.astype(jnp.bfloat16)
    low = (x - high.astype(np.float32)).astype(jnp.bfloat16)
    return jnp.asarray(high), jnp.asarray(low)


def rows_of(ref):
    count, planes, lanes = ref.shape
    return ref[...].reshape(count * planes, lanes)


def one_hot(shape, row, column):
    r = lax.broadcasted_iota(jnp.int32, shape, 0)
    c = lax.broadcasted_iota(jnp.int32, shape, 1)
    return (row(r) == column(c)).astype(jnp.float32)


def gram_kernel(slots, *refs):
    b_refs, l_ref, out_ref, acc_ref = refs[:slots], refs[slots], refs[slots + 1], refs[slots + 2]
    step = pl.program_id(0)
    planes = l_ref.shape[1]
    bh, bl = split(jnp.concatenate([rows_of(r) for r in b_refs], axis=0))
    lh, ll = split(rows_of(l_ref))
    rh = jnp.concatenate([bh, lh], axis=0)
    rl = jnp.concatenate([bl, ll], axis=0)
    nt = ((1,), (1,))
    part = dot(bh, rh, nt) + (dot(bh, rl, nt) + dot(bl, rh, nt))

    @pl.when(step == 0)
    def _():
        acc_ref[...] = part

    @pl.when(step > 0)
    def _():
        acc_ref[...] += part

    @pl.when(step == pl.num_programs(0) - 1)
    def _():
        full = acc_ref[...]
        m, n = full.shape
        full = full * one_hot((m, n), lambda r: r % planes, lambda c: c % planes)
        left = one_hot((m // planes, m), lambda r: r, lambda c: c // planes)
        right = one_hot((n, n // planes), lambda r: r // planes, lambda c: c)
        out_ref[...] = exact(exact(left, full), right)


def gram(slots, later):
    own, planes, length = slots[0].shape
    rows = own * len(slots)
    count = later.shape[0]
    lanes = 2 * GROUP
    along = lambda n: pl.BlockSpec((n, planes, lanes), lambda i: (0, 0, i))
    return pl.pallas_call(
        functools.partial(gram_kernel, len(slots)),
        grid=(length // lanes,),
        in_specs=[along(own)] * len(slots) + [along(count)],
        out_specs=pl.BlockSpec((rows, rows + count), lambda i: (0, 0)),
        out_shape=jax.ShapeDtypeStruct((rows, rows + count), jnp.float32),
        scratch_shapes=[pltpu.VMEM((rows * planes, (rows + count) * planes), jnp.float32)],
        compiler_params=pltpu.CompilerParams(vmem_limit_bytes=32 << 20),
        cost_estimate=pl.CostEstimate(
            flops=8_000_000_000, bytes_accessed=4 * (rows + count) * planes * length, transcendentals=0
        ),
        name="gram",
    )(*slots, later)


def mix_kernel(band_ref, slow_ref, prod_ref, m1h, m1l, m2h, m2l, work_ref, *, cells, bands, own_rows, count):
    rows = prod_ref.shape[0]
    block_rows = bands * own_rows
    own = 2 * own_rows
    planes = REACH
    band = band_ref[0]

    def home(r):
        slot, inside = r // own, r % own
        held = (slot + band) % bands
        return (inside // own_rows) * block_rows + held * own_rows + inside % own_rows

    place = one_hot((rows, rows), lambda r: r, home)
    products = exact(place, prod_ref[...] * (1.0 / cells))
    corr = exact(products[:, :rows], place, ((1,), (1,)))
    eye = one_hot((rows, rows), lambda r: r, lambda c: c)
    work_ref[...] = jnp.concatenate([corr, eye, products[:, rows:]], axis=1)
    width = work_ref.shape[1]
    row_id = lax.broadcasted_iota(jnp.int32, (rows, 1), 0)
    col_id = lax.broadcasted_iota(jnp.int32, (rows, width), 1)

    def eliminate(j, _):
        table = work_ref[...]
        pivot_row = work_ref[pl.ds(j, 1), :]
        column = jnp.sum(jnp.where(col_id == j, table, 0.0), axis=1, keepdims=True)
        pivot = jnp.sum(jnp.where(row_id == j, column, 0.0), axis=0, keepdims=True)
        scale = lax.rsqrt(pivot)
        scale = scale * (1.5 - 0.5 * pivot * scale * scale)
        scaled = pivot_row * scale
        factor = jnp.where(row_id > j, column * scale, 0.0)
        work_ref[...] = jnp.where(row_id == j, scaled, table - factor * scaled)
        return 0

    lax.fori_loop(0, rows, eliminate, 0)
    table = work_ref[...]
    inverse = table[:, rows : 2 * rows]
    weights = table[:, 2 * rows :]
    tn = ((0,), (0,))
    coefs = exact(weights, inverse, tn)
    mine = one_hot((own, rows), lambda r: (r // own_rows) * block_rows + band * own_rows + r % own_rows, lambda c: c)
    mix = jnp.concatenate([-coefs, exact(mine, inverse)], axis=0)
    mix = exact(mix, place)
    outs = count + own
    tall = one_hot((outs * planes, outs), lambda r: r // planes, lambda c: c)
    wide = one_hot((rows, rows * planes), lambda r: r, lambda c: c // planes)
    spread = exact(exact(tall, mix), wide)
    p = lax.broadcasted_iota(jnp.int32, spread.shape, 0) % planes
    q = lax.broadcasted_iota(jnp.int32, spread.shape, 1) % planes
    first = jnp.where(p == q, spread, 0.0)
    pattern = jnp.zeros_like(spread)
    for a in range(planes):
        for b in range(planes):
            pattern = jnp.where((p == a) & (q == b), slow_ref[a, b], pattern)
    second = spread * pattern
    m1h[...], m1l[...] = split(first)
    m2h[...], m2l[...] = split(second)


def mix(products, band, slow_mat, cells, bands, own_rows, count):
    rows = products.shape[0]
    planes = REACH
    out = jax.ShapeDtypeStruct(((count + 2 * own_rows) * planes, rows * planes), jnp.bfloat16)
    return pl.pallas_call(
        functools.partial(mix_kernel, cells=cells, bands=bands, own_rows=own_rows, count=count),
        in_specs=[
            pl.BlockSpec(memory_space=pltpu.SMEM),
            pl.BlockSpec(memory_space=pltpu.SMEM),
            pl.BlockSpec(memory_space=pltpu.VMEM),
        ],
        out_specs=[pl.BlockSpec(memory_space=pltpu.VMEM)] * 4,
        out_shape=[out] * 4,
        scratch_shapes=[pltpu.VMEM((rows, 2 * rows + count), jnp.float32)],
        compiler_params=pltpu.CompilerParams(vmem_limit_bytes=32 << 20),
        cost_estimate=pl.CostEstimate(flops=10_000_000_000, bytes_accessed=1 << 20, transcendentals=0),
        name="mix",
    )(band.reshape(1), slow_mat, products)


def along_y(x):
    n = len(x)
    lane = lax.broadcasted_iota(jnp.int32, (8, LANE), 1)
    zero = jnp.zeros((8, LANE), jnp.float32)
    r32 = [pltpu.roll(v, 32, 1) for v in x]
    r64 = [pltpu.roll(v, 64, 1) for v in x]
    r96 = [pltpu.roll(v, 96, 1) for v in x]
    at = lambda list_, i: list_[i] if 0 <= i < n else zero
    below32, below64, below96 = lane < 32, lane < 64, lane < 96
    out = []
    for i in range(n):
        one = jnp.where(below32, at(r32, i), at(r32, i + 1)) + jnp.where(below96, at(r96, i - 1), at(r96, i))
        two = jnp.where(below64, at(r64, i + 1), at(r64, i + 2)) + jnp.where(below64, at(r64, i - 2), at(r64, i - 1))
        three = jnp.where(below96, at(r96, i + 2), at(r96, i + 3)) + jnp.where(below32, at(r32, i - 3), at(r32, i - 2))
        four = at(x, i + 3) + at(x, i - 3)
        out.append(half_weights[1] * one + half_weights[2] * two + half_weights[3] * three + half_weights[4] * four)
    return out


def stencil_kernel(x_ref, halo_ref, mh_ref, ml_ref, zh_ref, zl_ref, v_ref, out_ref, flat_ref, acc_ref):
    count, planes, length = x_ref.shape
    rows = count * planes
    groups = length // GROUP
    flat_ref[...] = rows_of(x_ref)
    vectors = length // LANE

    def eight(t, _):
        at = pl.ds(pl.multiple_of(t * 8, 8), 8)
        x = [flat_ref[at, i * LANE : (i + 1) * LANE] for i in range(vectors)]
        ys = along_y(x)
        for i in range(vectors):
            acc_ref[at, i * LANE : (i + 1) * LANE] = ys[i] + v_ref[:, i * LANE : (i + 1) * LANE] * x[i]
        return 0

    lax.fori_loop(0, rows // 8, eight, 0)
    zh, zl = zh_ref[...], zl_ref[...]
    mh, ml = mh_ref[...], ml_ref[...]
    for g in range(groups):
        here = slice(g * GROUP, (g + 1) * GROUP)
        xh, xl = split(flat_ref[:, here])
        hh, hl = split(halo_ref[:, :, here].reshape(rows, GROUP))
        both_h = jnp.concatenate([xh, hh], axis=0)
        both_l = jnp.concatenate([xl, hl], axis=0)
        total = dot(xh, zh) + dot(mh, both_h)
        total += dot(xh, zl) + dot(mh, both_l)
        total += dot(xl, zh) + dot(ml, both_h)
        total += acc_ref[:, here]
        out_ref[:, :, here] = total.reshape(count, planes, GROUP)


def stencil(x, halo, odd, potential, block):
    count, planes, length = x.shape
    size = block * planes
    within = plane_matrix(0)
    mh, ml = split_constant(spread_variants([(within, plane_matrix(planes)), (within, plane_matrix(-planes))], block))
    zh, zl = split_constant(z_matrix())
    v = jnp.concatenate([potential, potential], axis=0)
    spec = pl.BlockSpec((block, planes, length), lambda i, odd: (i, 0, 0))
    picked = pl.BlockSpec((pl.squeezed,) + mh.shape[1:], lambda i, odd: (odd[0], 0, 0))
    fixed = lambda a: pl.BlockSpec(a.shape, lambda i, odd: (0, 0))
    return pl.pallas_call(
        lambda odd_ref, *refs: stencil_kernel(*refs),
        grid_spec=pltpu.PrefetchScalarGridSpec(
            num_scalar_prefetch=1,
            grid=(count // block,),
            in_specs=[spec, spec, picked, picked] + [fixed(a) for a in (zh, zl, v)],
            out_specs=spec,
            scratch_shapes=[pltpu.VMEM((size, length), jnp.float32)] * 2,
        ),
        out_shape=jax.ShapeDtypeStruct(x.shape, jnp.float32),
        compiler_params=pltpu.CompilerParams(vmem_limit_bytes=48 << 20),
        cost_estimate=pl.CostEstimate(flops=100_000_000 * count, bytes_accessed=12 * x.size, transcendentals=0),
        name="stencil",
    )(odd, x, halo, mh, ml, zh, zl, v)


def add_slow_kernel(kind_ref, two_ref, base_ref, one_hop_ref, two_hop_ref, mh_ref, ml_ref, out_ref):
    count, planes, lanes = base_ref.shape
    rows = count * planes
    halo = jnp.where(two_ref[0] > 0, two_hop_ref[...], one_hop_ref[...]).reshape(rows, lanes)
    hh, hl = split(halo)
    mh, ml = mh_ref[...], ml_ref[...]
    total = dot(mh, hh) + (dot(mh, hl) + dot(ml, hh))
    out_ref[...] = base_ref[...] + total.reshape(count, planes, lanes)


def add_slow(kind, two, base, one_hop, two_hop):
    count, planes, length = base.shape
    none = np.zeros((planes, planes), np.float32)
    mh, ml = split_constant(spread_variants([(plane_matrix(-planes),), (plane_matrix(planes),), (none,)], count))
    lanes = 2 * GROUP
    along = pl.BlockSpec((count, planes, lanes), lambda i, kind, two: (0, 0, i))
    picked = pl.BlockSpec((pl.squeezed,) + mh.shape[1:], lambda i, kind, two: (kind[0], 0, 0))
    return pl.pallas_call(
        add_slow_kernel,
        grid_spec=pltpu.PrefetchScalarGridSpec(
            num_scalar_prefetch=2,
            grid=(length // lanes,),
            in_specs=[along, along, along, picked, picked],
            out_specs=along,
        ),
        out_shape=jax.ShapeDtypeStruct(base.shape, jnp.float32),
        compiler_params=pltpu.CompilerParams(vmem_limit_bytes=32 << 20),
        cost_estimate=pl.CostEstimate(flops=3_000_000_000, bytes_accessed=16 * base.size, transcendentals=0),
        name="add_slow",
    )(kind, two, base, one_hop, two_hop, mh, ml)


def final_kernel(slots, base_ref, *refs):
    hb_refs, slow_refs = refs[:slots], refs[slots : 2 * slots]
    m1h, m1l, m2h, m2l, later_ref, block_ref = refs[2 * slots :]
    count, planes, lanes = base_ref.shape
    hh, hl = split(jnp.concatenate([rows_of(r) for r in hb_refs], axis=0))
    sh, sl = split(jnp.concatenate([rows_of(r) for r in slow_refs], axis=0))
    total = dot(m1h[...], hh) + dot(m2h[...], sh)
    total += dot(m1h[...], hl) + dot(m2h[...], sl)
    total += dot(m1l[...], hh) + dot(m2l[...], sh)
    later_ref[...] = base_ref[...] + total[: count * planes].reshape(count, planes, lanes)
    block_ref[...] = total[count * planes :].reshape(block_ref.shape)


def final(base, hb, slow, mats):
    count, planes, length = base.shape
    own = hb[0].shape[0]
    lanes = 2 * GROUP
    along = lambda n: pl.BlockSpec((n, planes, lanes), lambda i: (0, 0, i))
    fixed = pl.BlockSpec(mats[0].shape, lambda i: (0, 0))
    return pl.pallas_call(
        functools.partial(final_kernel, len(hb)),
        grid=(length // lanes,),
        in_specs=[along(count)] + [along(own)] * (2 * len(hb)) + [fixed] * 4,
        out_specs=[along(count), along(own)],
        out_shape=[
            jax.ShapeDtypeStruct((count, planes, length), jnp.float32),
            jax.ShapeDtypeStruct((own, planes, length), jnp.float32),
        ],
        compiler_params=pltpu.CompilerParams(vmem_limit_bytes=40 << 20),
        cost_estimate=pl.CostEstimate(flops=6_000_000_000, bytes_accessed=20 * base.size, transcendentals=0),
        name="final",
    )(base, *hb, *slow, *mats)


def after(x, *others):
    return lax.optimization_barrier((x,) + others)[0]


def local(blocks, later, potential):
    pair, own_rows, planes, length = blocks.shape
    count = later.shape[0]
    ns, nb = lax.axis_size("space"), lax.axis_size("band")
    s, band = lax.axis_index("space"), lax.axis_index("band")
    cells = planes * ns * length
    own = pair * own_rows
    both = ("space", "band")

    fast_pairs = [(i, i ^ 1) for i in range(ns)]
    near = [(i, i + 1) for i in range(1, ns - 1, 4)]
    near += [(j, i) for i, j in near]
    across = range(3, ns - 1, 4)
    far = [(i, i + 1) for i in across] + [(i + 1, i) for i in across]
    hop_one = [(i, i + 4) for i in across] + [(i + 1, i - 3) for i in across]
    hop_two = [(i + 4, i + 1) for i in across] + [(i - 3, i) for i in across]
    is_far = ((s % 4 == 3) & (s < ns - 1)) | ((s % 4 == 0) & (s > 0))
    ring = [(b + 1, b) for b in range(nb - 1)] + [(0, nb - 1)]
    far_pairs = [(i * nb + b, j * nb + b) for i, j in far for b in range(nb)]

    odd = (s % 2).astype(jnp.int32).reshape(1)
    edge = (s == 0) | (s == ns - 1)
    kind = jnp.where(edge, 2, odd)
    before, behind = plane_matrix(-planes), plane_matrix(planes)
    slow_mat = jnp.where(edge, 0.0, jnp.where(s % 2 == 0, before, behind))

    mine = blocks.reshape(own, planes, length)
    slots, slow = [None] * nb, [None] * nb
    slots[0] = mine
    up = lambda x: lax.ppermute(x, "band", ring)
    down = lambda x: lax.ppermute(x, "band", [(j, i) for i, j in ring])
    swap = lambda x: lax.ppermute(x, "space", fast_pairs)
    step_up = lambda x: lax.ppermute(x, both, far_pairs + [(i * nb + b, i * nb + c) for i, _ in near for b, c in ring])
    step_down = lambda x: lax.ppermute(x, both, far_pairs + [(i * nb + c, i * nb + b) for i, _ in near for b, c in ring])

    slots[1], slots[-1] = up(mine), down(mine)
    fast_later, fast_mine = swap(later), swap(mine)
    slow[0] = lax.ppermute(mine, "space", near + far)
    one_hop = lax.ppermute(later, "space", near + hop_one)
    base = stencil(later, fast_later, odd, potential, min(32, count))
    hb = [None] * nb
    hb[0] = stencil(mine, fast_mine, odd, potential, own)
    token = (base, hb[0])
    fast = [fast_mine] + [None] * (nb - 1)
    order = []
    lo, hi = 1, nb - 1
    while lo <= hi:
        order += [lo] if lo == hi else [lo, hi]
        lo, hi = lo + 1, hi - 1
    for k in order:
        if slots[k] is None:
            low = k <= nb // 2
            slots[k] = (up if low else down)(after(slots[k - 1] if low else slots[k + 1], *token))
    for k in order:
        fast[k] = swap(slots[k])
    two_hop = lax.ppermute(one_hop, "space", hop_two)
    gathered = slots[nb // 2]
    for k in order:
        low = k <= nb // 2
        kept = jnp.where(is_far, slots[k], slow[k - 1] if low else slow[(k + 1) % nb])
        slow[k] = (step_up if low else step_down)(after(kept, gathered))
    for k in order:
        hb[k] = stencil(slots[k], fast[k], odd, potential, own)

    products = gram(slots, later)
    reach = 1
    while reach < ns:
        products = products + lax.ppermute(products, "space", [(i, i ^ reach) for i in range(ns)])
        reach *= 2
    mats = mix(products, band, slow_mat, cells, nb, own_rows, count)
    base = add_slow(kind, is_far.astype(jnp.int32).reshape(1), base, one_hop, two_hop)
    h_later, h_block = final(base, hb, slow, mats)
    return h_block.reshape(blocks.shape), h_later


def solution(mesh):
    return jax.shard_map(
        local,
        mesh=mesh,
        in_specs=(P(None, "band", "space", None), P("band", "space", None), P("space", None)),
        out_specs=(P(None, "band", "space", None), P("band", "space", None)),
        check_vma=False,
    )
```

profile of v0, /device:TPU:6, one launch (start us, length us, event | category | flops | bytes accessed | tf_op | source)
XLA Modules:
  0.0 249.5 jit_solution(10938390335534290286)
XLA Ops:
  0.6 1.9 collective-permute-start.1
  3.1 3.6 %collective-permute-start.4 = (f32[16,4,6144]{2,1,0:T(4,128)}, f32[16,4,6144]{2,1,0:T(4,128)}, u32[]{:S(2)}, u32[]{:S(2)}) collective-permute-start(f32[16,4,6144]{2,1,0:T(4,128)} %bitcast.20), channel_id=1, source_target_pairs={{1,0},{2,1},{3,2},{0,3},{5,4},{6,5},{7,6},{4,7},{9,8},{10,9},{11,1... | collective-permute-start | bytes 4718600 | tf_op jit(solution)/shard_map/ppermute | solution.py:383
  6.7 6.4 %collective-permute-done.3.refs_1_ = f32[16,4,6144]{2,1,0:T(4,128)S(1)} collective-permute-done((f32[16,4,6144]{2,1,0:T(4,128)}, f32[16,4,6144]{2,1,0:T(4,128)S(1)}, u32[]{:S(2)}, u32[]{:S(2)}) %collective-permute-start.3) | collective-permute-done | bytes 1572896 | tf_op jit(solution)/shard_map/ppermute | solution.py:385
  13.1 4.5 %collective-permute-start.10 = (f32[16,4,6144]{2,1,0:T(4,128)}, f32[16,4,6144]{2,1,0:T(4,128)S(1)}, u32[]{:S(2)}, u32[]{:S(2)}) collective-permute-start(f32[16,4,6144]{2,1,0:T(4,128)} %bitcast.22), channel_id=1, source_target_pairs={{4,8},{20,24},{8,4},{24,20},{12,16},{16,12},{5,9},{21,25},{9,5},{2... | collective-permute-start | bytes 4718600 | tf_op jit(solution)/shard_map/ppermute | solution.py:391
  17.6 1.0 pad_maximum_fusion.refs_6_
  18.7 1.4 copy-done.6
  23.5 5.4 %stencil.6.refs_0_ = f32[16,4,6144]{2,1,0:T(4,128)S(1)} custom-call(s32[1]{0:T(128)} %bitcast.1.odd_ref, f32[16,4,6144]{2,1,0:T(4,128)S(1)} %bitcast.23, f32[16,4,6144]{2,1,0:T(4,128)S(1)} %collective-permute-done.3.refs_1_, bf16[2,64,128]{2,1,0:T(8,128)(2,1)S(1)} %copy-done.15, bf16[2,64,128]{2,1,0:T(8,128)(2,1)S(1)} %copy-done.17, ...), custom_call_target="tpu_custom_call" | custom-call | flops 1600000000 | bytes 4718592 | tf_op jit(solution)/shard_map/stencil/pallas_call | solution.py:268
  28.9 61.2 %collective-permute-done.1.one_hop_ref = f32[64,4,6144]{2,1,0:T(4,128)} collective-permute-done((f32[64,4,6144]{2,1,0:T(4,128)}, f32[64,4,6144]{2,1,0:T(4,128)}, u32[]{:S(2)}, u32[]{:S(2)}) %collective-permute-start.1) | collective-permute-done | bytes 6291488 | tf_op jit(solution)/shard_map/ppermute | solution.py:392
  90.1 3.3 %collective-permute-start.2 = (f32[64,4,6144]{2,1,0:T(4,128)}, f32[64,4,6144]{2,1,0:T(4,128)}, u32[]{:S(2)}, u32[]{:S(2)}) collective-permute-start(f32[64,4,6144]{2,1,0:T(4,128)} %collective-permute-done.1.one_hop_ref), channel_id=1, source_target_pairs={{28,16},{0,12},{29,17},{1,13},{30,18},{2,14},{31,19},{3,15}} | collective-permute-start | bytes 18874376 | tf_op jit(solution)/shard_map/ppermute | solution.py:409
  93.5 23.1 %stencil.5.base_ref = f32[64,4,6144]{2,1,0:T(4,128)} custom-call(s32[1]{0:T(128)} %bitcast.1.odd_ref, f32[64,4,6144]{2,1,0:T(4,128)} %refs_4_.6, f32[64,4,6144]{2,1,0:T(4,128)} %collective-permute-done.refs_1_, bf16[2,128,256]{2,1,0:T(8,128)(2,1)S(1)} %copy-done.13, bf16[2,128,256]{2,1,0:T(8,128)(2,1)S(1)} %copy-done.14, bf16[384,384]{1,0:T(8,128)(2,1)S(1)} %copy-done.9, ...), custom_call_target="tpu_custom_call" | custom-call | flops 6400000000 | bytes 18874368 | tf_op jit(solution)/shard_map/stencil/pallas_call | solution.py:268
  116.6 3.6 %collective-permute-start.6 = (f32[16,4,6144]{2,1,0:T(4,128)}, f32[16,4,6144]{2,1,0:T(4,128)S(1)}, u32[]{:S(2)}, u32[]{:S(2)}) collective-permute-start(f32[16,4,6144]{2,1,0:T(4,128)} %collective-permute-done.4.refs_0_.refs_1_), channel_id=1, source_target_pairs={{1,0},{2,1},{3,2},{0,3},{5,4},{6,5},{7,6},{4,7},{9,8},{10,9},{11,1... | collective-permute-start | bytes 4718600 | tf_op jit(solution)/shard_map/ppermute | solution.py:383
  120.3 2.1 broadcast_select_fusion
  122.4 16.1 %collective-permute-done.6.refs_0_.refs_2_ = f32[16,4,6144]{2,1,0:T(4,128)S(1)} collective-permute-done((f32[16,4,6144]{2,1,0:T(4,128)}, f32[16,4,6144]{2,1,0:T(4,128)S(1)}, u32[]{:S(2)}, u32[]{:S(2)}) %collective-permute-start.6) | collective-permute-done | bytes 1572896 | tf_op jit(solution)/shard_map/ppermute | solution.py:383
  138.5 6.1 %collective-permute-start.11 = (f32[16,4,6144]{2,1,0:T(4,128)}, f32[16,4,6144]{2,1,0:T(4,128)S(1)}, u32[]{:S(2)}, u32[]{:S(2)}) collective-permute-start(f32[16,4,6144]{2,1,0:T(4,128)} %bitcast.10), channel_id=1, source_target_pairs={{12,16},{13,17},{14,18},{15,19},{16,12},{17,13},{18,14},{19,15},{5... | collective-permute-start | bytes 4718600 | tf_op jit(solution)/shard_map/ppermute | solution.py:386
  144.7 2.8 %copy-done.5 = f32[64,4,6144]{2,1,0:T(4,128)S(1)} copy-done((f32[64,4,6144]{2,1,0:T(4,128)S(1)}, f32[64,4,6144]{2,1,0:T(4,128)}, u32[]{:S(2)}) %copy-start.5) | copy-done | bytes 6291480
  147.5 1.4 copy-done.7
  148.9 9.4 %gram.1 = f32[64,128]{1,0:T(8,128)S(1)} custom-call(f32[16,4,6144]{2,1,0:T(4,128)S(1)} %bitcast.24, f32[16,4,6144]{2,1,0:T(4,128)} %collective-permute-done.4.refs_0_.refs_1_, f32[16,4,6144]{2,1,0:T(4,128)S(1)} %collective-permute-done.6.refs_0_.refs_2_, f32[16,4,6144]{2,1,0:T(4,128)} %collective-permute-done.8.refs_0_.refs_3_, f32[64,4,6144]{2,1,0:T(4,128)S(1)} %copy-done.5), custom_call_target="tpu_custom_call" | custom-call | flops 8000000000 | bytes 12582912 | tf_op jit(solution)/shard_map/gram/pallas_call | solution.py:115
  160.0 2.8 %collective-permute-done.11.refs_5_ = f32[16,4,6144]{2,1,0:T(4,128)S(1)} collective-permute-done((f32[16,4,6144]{2,1,0:T(4,128)}, f32[16,4,6144]{2,1,0:T(4,128)S(1)}, u32[]{:S(2)}, u32[]{:S(2)}) %collective-permute-start.11) | collective-permute-done | bytes 1572896 | tf_op jit(solution)/shard_map/ppermute | solution.py:386
  162.8 1.3 broadcast_select_fusion.1
  164.2 1.9 collective-permute-start.13
  166.7 6.1 %collective-permute-start.12 = (f32[16,4,6144]{2,1,0:T(4,128)}, f32[16,4,6144]{2,1,0:T(4,128)}, u32[]{:S(2)}, u32[]{:S(2)}) collective-permute-start(f32[16,4,6144]{2,1,0:T(4,128)} %bitcast.13), channel_id=1, source_target_pairs={{12,16},{13,17},{14,18},{15,19},{16,12},{17,13},{18,14},{19,15},{5... | collective-permute-start | bytes 4718600 | tf_op jit(solution)/shard_map/ppermute | solution.py:386
  172.8 7.4 %stencil.7.refs_1_ = f32[16,4,6144]{2,1,0:T(4,128)S(1)} custom-call(s32[1]{0:T(128)} %bitcast.1.odd_ref, f32[16,4,6144]{2,1,0:T(4,128)} %collective-permute-done.4.refs_0_.refs_1_, f32[16,4,6144]{2,1,0:T(4,128)} %collective-permute-done.5.refs_1_, bf16[2,64,128]{2,1,0:T(8,128)(2,1)S(1)} %copy-done.16, bf16[2,64,128]{2,1,0:T(8,128)(2,1)S(1)} %copy-done.18, ...), custom_call_target="tpu_custom_call" | custom-call | flops 1600000000 | bytes 4718592 | tf_op jit(solution)/shard_map/stencil/pallas_call | solution.py:268
  180.3 1.1 copy-done.21
  181.5 6.8 %stencil.9.refs_3_ = f32[16,4,6144]{2,1,0:T(4,128)S(1)} custom-call(s32[1]{0:T(128)} %bitcast.1.odd_ref, f32[16,4,6144]{2,1,0:T(4,128)} %collective-permute-done.8.refs_0_.refs_3_, f32[16,4,6144]{2,1,0:T(4,128)S(1)} %collective-permute-done.9.refs_1_, bf16[2,64,128]{2,1,0:T(8,128)(2,1)S(1)} %copy-done.16, bf16[2,64,128]{2,1,0:T(8,128)(2,1)S(1)} %copy-done.18, ...), custom_call_target="tpu_custom_call" | custom-call | flops 1600000000 | bytes 4718592 | tf_op jit(solution)/shard_map/stencil/pallas_call | solution.py:268
  188.3 14.9 %collective-permute-done.16 = f32[64,128]{1,0:T(8,128)S(1)} collective-permute-done((f32[64,128]{1,0:T(8,128)S(1)}, f32[64,128]{1,0:T(8,128)S(1)}, u32[]{:S(2)}, u32[]{:S(2)}) %collective-permute-start.16) | collective-permute-done | bytes 32800 | tf_op jit(solution)/shard_map/ppermute | solution.py:421
  203.2 10.4 %mix.1 = (bf16[320,256]{1,0:T(8,128)(2,1)S(1)}, bf16[320,256]{1,0:T(8,128)(2,1)S(1)}, bf16[320,256]{1,0:T(8,128)(2,1)S(1)}, bf16[320,256]{1,0:T(8,128)(2,1)S(1)}) custom-call(s32[1]{0:T(128)} %bitcast.4.band_ref, f32[4,4]{1,0:T(4,128)S(1)} %select_select_fusion.slow_ref, f32[64,128]{1,0:T(8,128)S(1)} %add.22.prod_ref), custom_call_target="tpu_custom_call" | custom-call | flops 10000000000 | bytes 1048576 | tf_op jit(solution)/shard_map/mix/pallas_call | solution.py:192
  215.0 6.9 %stencil.8.refs_2_ = f32[16,4,6144]{2,1,0:T(4,128)S(1)} custom-call(s32[1]{0:T(128)} %bitcast.1.odd_ref, f32[16,4,6144]{2,1,0:T(4,128)S(1)} %collective-permute-done.6.refs_0_.refs_2_, f32[16,4,6144]{2,1,0:T(4,128)} %collective-permute-done.7.refs_1_, bf16[2,64,128]{2,1,0:T(8,128)(2,1)S(1)} %copy-done.16, bf16[2,64,128]{2,1,0:T(8,128)(2,1)S(1)} %copy-done.18, ...), custom_call_target="tpu_custom_call" | custom-call | flops 1600000000 | bytes 4718592 | tf_op jit(solution)/shard_map/stencil/pallas_call | solution.py:268
  222.0 9.9 %add_slow.1.base_ref = f32[64,4,6144]{2,1,0:T(4,128)S(1)} custom-call(s32[1]{0:T(128)S(6)} %select_n.57.kind_ref, s32[1]{0:T(128)} %bitcast.2.two_ref, f32[64,4,6144]{2,1,0:T(4,128)S(1)} %bitcast.15, f32[64,4,6144]{2,1,0:T(4,128)} %collective-permute-done.1.one_hop_ref, f32[64,4,6144]{2,1,0:T(4,128)} %collective-permute-done.2.two_hop_ref, ...), custom_call_target="tpu_custom_call" | custom-call | flops 3000000000 | bytes 25165824 | tf_op jit(solution)/shard_map/add_slow/pallas_call | solution.py:301
  231.9 2.7 %copy-done = f32[64,4,6144]{2,1,0:T(4,128)} copy-done((f32[64,4,6144]{2,1,0:T(4,128)}, f32[64,4,6144]{2,1,0:T(4,128)S(1)}, u32[]{:S(2)}) %copy-start) | copy-done | bytes 6291480
  234.7 1.4 copy-done.22
  236.1 1.4 copy-done.26
  237.5 12.0 %final.1 = (f32[64,4,6144]{2,1,0:T(4,128)}, f32[16,4,6144]{2,1,0:T(4,128)}) custom-call(f32[64,4,6144]{2,1,0:T(4,128)} %copy-done, f32[16,4,6144]{2,1,0:T(4,128)S(1)} %copy-done.20, f32[16,4,6144]{2,1,0:T(4,128)S(1)} %copy-done.22, f32[16,4,6144]{2,1,0:T(4,128)S(1)} %copy-done.26, f32[16,4,6144]{2,1,0:T(4,128)S(1)} %copy-done.24, ...), custom_call_target="tpu_custom_call" | custom-call | flops 6000000000 | bytes 31457280 | tf_op jit(solution)/shard_map/final/pallas_call | solution.py:335
  (93 shorter events, 8.1 us)
Async XLA Ops:
  0.6 89.5 %collective-permute-start.1 = (f32[64,4,6144]{2,1,0:T(4,128)}, f32[64,4,6144]{2,1,0:T(4,128)}, u32[]{:S(2)}, u32[]{:S(2)}) collective-permute-start(f32[64,4,6144]{2,1,0:T(4,128)} %refs_4_.6), channel_id=1, source_target_pairs={{4,8},{20,24},{8,4},{24,20},{12,28},{16,0},{5,9},{21,25},{9,5},{25... | collective-permute-start | bytes 18874376 | tf_op jit(solution)/shard_map/ppermute | solution.py:392
  2.6 90.9 %collective-permute-start = (f32[64,4,6144]{2,1,0:T(4,128)}, f32[64,4,6144]{2,1,0:T(4,128)}, u32[]{:S(2)}, u32[]{:S(2)}) collective-permute-start(f32[64,4,6144]{2,1,0:T(4,128)} %refs_4_.6), channel_id=1, source_target_pairs={{0,4},{4,0},{8,12},{12,8},{16,20},{20,16},{24,28},{28,24},{1,5},{5... | collective-permute-start | bytes 18874376 | tf_op jit(solution)/shard_map/ppermute | solution.py:385
  2.6 10.5 %collective-permute-start.3 = (f32[16,4,6144]{2,1,0:T(4,128)}, f32[16,4,6144]{2,1,0:T(4,128)S(1)}, u32[]{:S(2)}, u32[]{:S(2)}) collective-permute-start(f32[16,4,6144]{2,1,0:T(4,128)} %bitcast.19), channel_id=1, source_target_pairs={{0,4},{4,0},{8,12},{12,8},{16,20},{20,16},{24,28},{28,24},{1,5},{5... | collective-permute-start | bytes 4718600 | tf_op jit(solution)/shard_map/ppermute | solution.py:385
  3.1 113.5 %collective-permute-start.4 = (f32[16,4,6144]{2,1,0:T(4,128)}, f32[16,4,6144]{2,1,0:T(4,128)}, u32[]{:S(2)}, u32[]{:S(2)}) collective-permute-start(f32[16,4,6144]{2,1,0:T(4,128)} %bitcast.20), channel_id=1, source_target_pairs={{1,0},{2,1},{3,2},{0,3},{5,4},{6,5},{7,6},{4,7},{9,8},{10,9},{11,1... | collective-permute-start | bytes 4718600 | tf_op jit(solution)/shard_map/ppermute | solution.py:383
  6.7 113.5 %collective-permute-start.8 = (f32[16,4,6144]{2,1,0:T(4,128)}, f32[16,4,6144]{2,1,0:T(4,128)}, u32[]{:S(2)}, u32[]{:S(2)}) collective-permute-start(f32[16,4,6144]{2,1,0:T(4,128)} %bitcast.21), channel_id=1, source_target_pairs={{0,1},{1,2},{2,3},{3,0},{4,5},{5,6},{6,7},{7,4},{8,9},{9,10},{10,1... | collective-permute-start | bytes 4718600 | tf_op jit(solution)/shard_map/ppermute | solution.py:384
  13.1 107.1 %collective-permute-start.10 = (f32[16,4,6144]{2,1,0:T(4,128)}, f32[16,4,6144]{2,1,0:T(4,128)S(1)}, u32[]{:S(2)}, u32[]{:S(2)}) collective-permute-start(f32[16,4,6144]{2,1,0:T(4,128)} %bitcast.22), channel_id=1, source_target_pairs={{4,8},{20,24},{8,4},{24,20},{12,16},{16,12},{5,9},{21,25},{9,5},{2... | collective-permute-start | bytes 4718600 | tf_op jit(solution)/shard_map/ppermute | solution.py:391
  23.5 70.0 %copy-start.9 = (bf16[384,384]{1,0:T(8,128)(2,1)S(1)}, bf16[384,384]{1,0:T(8,128)(2,1)}, u32[]{:S(2)}) copy-start(bf16[384,384]{1,0:T(8,128)(2,1)} %constant.68.clone.refs_4_) | copy-start | bytes 884740
  23.5 70.0 %copy-start.13 = (bf16[2,128,256]{2,1,0:T(8,128)(2,1)S(1)}, bf16[2,128,256]{2,1,0:T(8,128)(2,1)}, u32[]{:S(2)}) copy-start(bf16[2,128,256]{2,1,0:T(8,128)(2,1)} %constant.66.clone.refs_2_) | copy-start | bytes 393220
  23.5 70.0 %copy-start.14 = (bf16[2,128,256]{2,1,0:T(8,128)(2,1)S(1)}, bf16[2,128,256]{2,1,0:T(8,128)(2,1)}, u32[]{:S(2)}) copy-start(bf16[2,128,256]{2,1,0:T(8,128)(2,1)} %constant.67.clone.refs_3_) | copy-start | bytes 393220
  28.9 87.7 %copy-start.19 = (f32[16,4,6144]{2,1,0:T(4,128)}, f32[16,4,6144]{2,1,0:T(4,128)S(1)}, u32[]{:S(2)}) copy-start(f32[16,4,6144]{2,1,0:T(4,128)S(1)} %stencil.6.refs_0_) | copy-start | bytes 4718596
  90.1 131.7 %collective-permute-start.2 = (f32[64,4,6144]{2,1,0:T(4,128)}, f32[64,4,6144]{2,1,0:T(4,128)}, u32[]{:S(2)}, u32[]{:S(2)}) collective-permute-start(f32[64,4,6144]{2,1,0:T(4,128)} %collective-permute-done.1.one_hop_ref), channel_id=1, source_target_pairs={{28,16},{0,12},{29,17},{1,13},{30,18},{2,14},{31,19},{3,15}} | collective-permute-start | bytes 18874376 | tf_op jit(solution)/shard_map/ppermute | solution.py:409
  116.6 21.9 %collective-permute-start.6 = (f32[16,4,6144]{2,1,0:T(4,128)}, f32[16,4,6144]{2,1,0:T(4,128)S(1)}, u32[]{:S(2)}, u32[]{:S(2)}) collective-permute-start(f32[16,4,6144]{2,1,0:T(4,128)} %collective-permute-done.4.refs_0_.refs_1_), channel_id=1, source_target_pairs={{1,0},{2,1},{3,2},{0,3},{5,4},{6,5},{7,6},{4,7},{9,8},{10,9},{11,1... | collective-permute-start | bytes 4718600 | tf_op jit(solution)/shard_map/ppermute | solution.py:383
  138.5 24.3 %collective-permute-start.11 = (f32[16,4,6144]{2,1,0:T(4,128)}, f32[16,4,6144]{2,1,0:T(4,128)S(1)}, u32[]{:S(2)}, u32[]{:S(2)}) collective-permute-start(f32[16,4,6144]{2,1,0:T(4,128)} %bitcast.10), channel_id=1, source_target_pairs={{12,16},{13,17},{14,18},{15,19},{16,12},{17,13},{18,14},{19,15},{5... | collective-permute-start | bytes 4718600 | tf_op jit(solution)/shard_map/ppermute | solution.py:386
  144.6 19.6 %collective-permute-start.5 = (f32[16,4,6144]{2,1,0:T(4,128)}, f32[16,4,6144]{2,1,0:T(4,128)}, u32[]{:S(2)}, u32[]{:S(2)}) collective-permute-start(f32[16,4,6144]{2,1,0:T(4,128)} %collective-permute-done.4.refs_0_.refs_1_), channel_id=1, source_target_pairs={{0,4},{4,0},{8,12},{12,8},{16,20},{20,16},{24,28},{28,24},{1,5},{5... | collective-permute-start | bytes 4718600 | tf_op jit(solution)/shard_map/ppermute | solution.py:385
  158.3 1.4 collective-permute-start.14
  158.8 22.6 %collective-permute-start.9 = (f32[16,4,6144]{2,1,0:T(4,128)}, f32[16,4,6144]{2,1,0:T(4,128)S(1)}, u32[]{:S(2)}, u32[]{:S(2)}) collective-permute-start(f32[16,4,6144]{2,1,0:T(4,128)} %collective-permute-done.8.refs_0_.refs_3_), channel_id=1, source_target_pairs={{0,4},{4,0},{8,12},{12,8},{16,20},{20,16},{24,28},{28,24},{1,5},{5... | collective-permute-start | bytes 4718600 | tf_op jit(solution)/shard_map/ppermute | solution.py:385
  159.7 55.3 %collective-permute-start.7 = (f32[16,4,6144]{2,1,0:T(4,128)S(1)}, f32[16,4,6144]{2,1,0:T(4,128)}, u32[]{:S(2)}, u32[]{:S(2)}) collective-permute-start(f32[16,4,6144]{2,1,0:T(4,128)S(1)} %collective-permute-done.6.refs_0_.refs_2_), channel_id=1, source_target_pairs={{0,4},{4,0},{8,12},{12,8},{16,20},{20,16},{24,28},{28,24},{1,5},{5... | collective-permute-start | bytes 4718600 | tf_op jit(solution)/shard_map/ppermute | solution.py:385
  162.8 3.9 %collective-permute-start.15 = (f32[64,128]{1,0:T(8,128)S(1)}, f32[64,128]{1,0:T(8,128)S(1)}, u32[]{:S(2)}, u32[]{:S(2)}) collective-permute-start(f32[64,128]{1,0:T(8,128)S(1)} %add.20), channel_id=1, source_target_pairs={{0,8},{4,12},{8,0},{12,4},{16,24},{20,28},{24,16},{28,20},{1,9},{5... | collective-permute-start | bytes 98312 | tf_op jit(solution)/shard_map/ppermute | solution.py:421
  162.8 10.0 %copy-start.18 = (bf16[2,64,128]{2,1,0:T(8,128)(2,1)S(1)}, bf16[2,64,128]{2,1,0:T(8,128)(2,1)}, u32[]{:S(2)}) copy-start(bf16[2,64,128]{2,1,0:T(8,128)(2,1)} %constant.71.clone.refs_3_) | copy-start | bytes 98308
  164.2 70.4 %collective-permute-start.13 = (f32[16,4,6144]{2,1,0:T(4,128)}, f32[16,4,6144]{2,1,0:T(4,128)}, u32[]{:S(2)}, u32[]{:S(2)}) collective-permute-start(f32[16,4,6144]{2,1,0:T(4,128)} %bitcast.9), channel_id=1, source_target_pairs={{12,16},{13,17},{14,18},{15,19},{16,12},{17,13},{18,14},{19,15},{4... | collective-permute-start | bytes 4718600 | tf_op jit(solution)/shard_map/ppermute | solution.py:387
  166.7 67.9 %collective-permute-start.12 = (f32[16,4,6144]{2,1,0:T(4,128)}, f32[16,4,6144]{2,1,0:T(4,128)}, u32[]{:S(2)}, u32[]{:S(2)}) collective-permute-start(f32[16,4,6144]{2,1,0:T(4,128)} %bitcast.13), channel_id=1, source_target_pairs={{12,16},{13,17},{14,18},{15,19},{16,12},{17,13},{18,14},{19,15},{5... | collective-permute-start | bytes 4718600 | tf_op jit(solution)/shard_map/ppermute | solution.py:386
  181.4 21.8 %collective-permute-start.16 = (f32[64,128]{1,0:T(8,128)S(1)}, f32[64,128]{1,0:T(8,128)S(1)}, u32[]{:S(2)}, u32[]{:S(2)}) collective-permute-start(f32[64,128]{1,0:T(8,128)S(1)} %add.21), channel_id=1, source_target_pairs={{0,16},{4,20},{8,24},{12,28},{16,0},{20,4},{24,8},{28,12},{1,17},{... | collective-permute-start | bytes 98312 | tf_op jit(solution)/shard_map/ppermute | solution.py:421
  188.3 25.3 %copy-start.23 = (f32[16,4,6144]{2,1,0:T(4,128)}, f32[16,4,6144]{2,1,0:T(4,128)S(1)}, u32[]{:S(2)}) copy-start(f32[16,4,6144]{2,1,0:T(4,128)S(1)} %stencil.9.refs_3_) | copy-start | bytes 4718596
  203.2 18.6 %slice-start = ((s8[6291456]{0:T(1024)(128)(4,1)}), s8[4194304]{0:T(1024)(128)(4,1)S(1)}, s32[]{:S(2)}) async-start(s8[6291456]{0:T(1024)(128)(4,1)} %bitcast.14), calls=%async_computation | async-start | bytes 8388608
  203.2 18.6 %slice-start.1 = ((s8[6291456]{0:T(1024)(128)(4,1)}), s8[2097152]{0:T(1024)(128)(4,1)S(1)}, s32[]{:S(2)}) async-start(s8[6291456]{0:T(1024)(128)(4,1)} %bitcast.14), calls=%async_computation.1 | async-start | bytes 4194304
  221.8 10.1 %copy-start.25 = (f32[16,4,6144]{2,1,0:T(4,128)}, f32[16,4,6144]{2,1,0:T(4,128)S(1)}, u32[]{:S(2)}) copy-start(f32[16,4,6144]{2,1,0:T(4,128)S(1)} %stencil.8.refs_2_) | copy-start | bytes 4718596
  221.9 12.7 %copy-start.2 = (f32[16,4,6144]{2,1,0:T(4,128)S(1)}, f32[16,4,6144]{2,1,0:T(4,128)}, u32[]{:S(2)}) copy-start(f32[16,4,6144]{2,1,0:T(4,128)} %copy-done.1) | copy-start | bytes 4718596
  221.9 12.7 %copy-start.20 = (f32[16,4,6144]{2,1,0:T(4,128)S(1)}, f32[16,4,6144]{2,1,0:T(4,128)}, u32[]{:S(2)}) copy-start(f32[16,4,6144]{2,1,0:T(4,128)} %copy-done.19) | copy-start | bytes 4718596
  221.9 12.7 %copy-start.24 = (f32[16,4,6144]{2,1,0:T(4,128)S(1)}, f32[16,4,6144]{2,1,0:T(4,128)}, u32[]{:S(2)}) copy-start(f32[16,4,6144]{2,1,0:T(4,128)} %copy-done.23) | copy-start | bytes 4718596
  221.9 12.7 %copy-start.28 = (bf16[320,256]{1,0:T(8,128)(2,1)S(1)}, bf16[320,256]{1,0:T(8,128)(2,1)}, u32[]{:S(2)}) copy-start(bf16[320,256]{1,0:T(8,128)(2,1)} %copy-done.27) | copy-start | bytes 491524
  221.9 12.7 %copy-start.30 = (bf16[320,256]{1,0:T(8,128)(2,1)S(1)}, bf16[320,256]{1,0:T(8,128)(2,1)}, u32[]{:S(2)}) copy-start(bf16[320,256]{1,0:T(8,128)(2,1)} %copy-done.29) | copy-start | bytes 491524
  222.0 12.7 %copy-start.32 = (bf16[320,256]{1,0:T(8,128)(2,1)S(1)}, bf16[320,256]{1,0:T(8,128)(2,1)}, u32[]{:S(2)}) copy-start(bf16[320,256]{1,0:T(8,128)(2,1)} %copy-done.31) | copy-start | bytes 491524
  (22 other events, 89.8 us)
where the time goes:
time: 254 us; the launch traced here: 250 us
  waiting for transfers between devices  103 us (41%)
  Pallas kernels  91.3 us (36%)
  starting transfers between devices  32.7 us (13%)
  local copies, waits for them, and re-layouts  17.1 us (7%)
  other arithmetic  4.44 us (2%)
    ppermute x1, waiting for transfers between devices, local(): one_hop = lax.ppermute(later, 'space', near + hop_one)  61.2 us
    pallas_call x5, Pallas kernels, stencil(): pl.pallas_call(lambda odd_ref, *refs: stencil_kernel(*refs), grid_spec=pl...  49.6 us
    unnamed x74, local copies, waits for them, and re-layouts  17.1 us
    ppermute x3, waiting for transfers between devices, local(): lax.ppermute(products, 'space', [(i, i ^ reach) for i in range(ns)])  16.3 us
    ppermute x2, waiting for transfers between devices, local(): up = lambda x: lax.ppermute(x, 'band', ring)  16.1 us
    ppermute x2, starting transfers between devices, local(): lax.ppermute(x, both, far_pairs + [(i * nb + b, i * nb + c) for i, _ in n...  12.1 us
    pallas_call x1, Pallas kernels, final(): pl.pallas_call(functools.partial(final_kernel, len(hb)), grid=(length //...  12 us
    pallas_call x1, Pallas kernels, mix(): pl.pallas_call(functools.partial(mix_kernel, cells=cells, bands=bands, ow...  10.4 us
  transfers between devices with their start and end apart: 17, of which 7 were waited for; matrix products, arithmetic and copies ran while one was open for 2% of the time, Pallas kernels for 32%

commit v1 on v0

v1 whole, which is shorter than its diff:
```python
import functools

import jax
import jax.numpy as jnp
import numpy as np
from jax import lax
from jax.experimental import pallas as pl
from jax.experimental.pallas import tpu as pltpu
from jax.sharding import PartitionSpec as P

NZ = 96
REACH = 4
LANE = 128
VMEM = 60 << 20

stencil_weights = (-205.0 / 72.0, 8.0 / 5.0, -1.0 / 5.0, 8.0 / 315.0, -1.0 / 560.0)
half_weights = tuple(-0.5 * w for w in stencil_weights)

GROUP = 4 * NZ
HIGHEST = lax.Precision.HIGHEST


def split(x):
    high = x.astype(jnp.bfloat16)
    low = (x - high.astype(jnp.float32)).astype(jnp.bfloat16)
    return high, low


def thrice(m):
    high, low = split(m)
    return jnp.concatenate([high, high, low], axis=1)


def stacked(x):
    high, low = split(x)
    return jnp.concatenate([high, low, high], axis=0)


def dot(a, b, dims=((1,), (0,))):
    return lax.dot_general(a, b, (dims, ((), ())), preferred_element_type=jnp.float32)


def exact(a, b, dims=((1,), (0,))):
    return lax.dot_general(a, b, (dims, ((), ())), precision=HIGHEST, preferred_element_type=jnp.float32)


def plane_matrix(offset):
    out = np.zeros((REACH, REACH), np.float32)
    for p in range(REACH):
        for q in range(REACH):
            shift = abs(q + offset - p)
            if 1 <= shift <= REACH:
                out[p, q] = half_weights[shift]
    return out


def spread_variants(left_of_variant, count):
    eye = np.eye(count, dtype=np.float32)
    return np.stack([np.concatenate([np.kron(eye, m) for m in ms], axis=1) for ms in left_of_variant])


def z_matrix():
    a = np.arange(GROUP)[:, None]
    o = np.arange(GROUP)[None, :]
    dz = np.abs(a - o)
    same = a // NZ == o // NZ
    out = np.zeros((GROUP, GROUP), np.float64)
    for step in range(1, REACH + 1):
        out += half_weights[step] * (same & (dz == step))
    out += 3.0 * half_weights[0] * (dz == 0)
    return out.astype(np.float32)


def thrice_constant(x):
    high = x.astype(jnp.bfloat16)
    low = (x - high.astype(np.float32)).astype(jnp.bfloat16)
    return jnp.asarray(np.concatenate([high, high, low], axis=-1))


def split_constant(x):
    high = x.astype(jnp.bfloat16)
    low = (x - high.astype(np.float32)).astype(jnp.bfloat16)
    return jnp.asarray(high), jnp.asarray(low)


def rows_of(ref):
    count, planes, lanes = ref.shape
    return ref[...].reshape(count * planes, lanes)


def one_hot(shape, row, column):
    r = lax.broadcasted_iota(jnp.int32, shape, 0)
    c = lax.broadcasted_iota(jnp.int32, shape, 1)
    return (row(r) == column(c)).astype(jnp.float32)


def gram_kernel(slots, *refs):
    b_refs, l_ref, out_ref, acc_ref = refs[:slots], refs[slots], refs[slots + 1], refs[slots + 2]
    step = pl.program_id(0)
    own, planes = b_refs[0].shape[:2]
    bh, bl = split(jnp.concatenate([rows_of(r) for r in b_refs], axis=0))
    lh, ll = split(rows_of(l_ref))
    rh = jnp.concatenate([bh, lh], axis=0)
    rl = jnp.concatenate([bl, ll], axis=0)
    part = dot(jnp.concatenate([bh, bh, bl], axis=1), jnp.concatenate([rh, rl, rh], axis=1), ((1,), (1,)))

    @pl.when(step == 0)
    def _():
        acc_ref[...] = part

    @pl.when(step > 0)
    def _():
        acc_ref[...] += part

    @pl.when(step == pl.num_programs(0) - 1)
    def _():
        full = acc_ref[...]
        m, n = full.shape
        full = full * one_hot((m, n), lambda r: r % planes, lambda c: c % planes)
        left = one_hot((m // planes, m), lambda r: r, lambda c: c // planes)
        place = lambda r: r // planes + jnp.where(r // planes < own * slots, 0, own)
        right = one_hot((n, out_ref.shape[1]), place, lambda c: c)
        out_ref[...] = exact(exact(left, full), right)


def gram(slots, later):
    own, planes, length = slots[0].shape
    rows = own * len(slots)
    count = later.shape[0]
    lanes = 2 * GROUP
    along = lambda n: pl.BlockSpec((n, planes, lanes), lambda i: (0, 0, i))
    return pl.pallas_call(
        functools.partial(gram_kernel, len(slots)),
        grid=(length // lanes,),
        in_specs=[along(own)] * len(slots) + [along(count)],
        out_specs=pl.BlockSpec((rows, rows + own + count), lambda i: (0, 0)),
        out_shape=jax.ShapeDtypeStruct((rows, rows + own + count), jnp.float32),
        scratch_shapes=[pltpu.VMEM((rows * planes, (rows + count) * planes), jnp.float32)],
        compiler_params=pltpu.CompilerParams(vmem_limit_bytes=VMEM),
        cost_estimate=pl.CostEstimate(
            flops=8_000_000_000, bytes_accessed=4 * (rows + count) * planes * length, transcendentals=0
        ),
        name="gram",
    )(*slots, later)


def gram_last_kernel(slots, *refs):
    b_refs, l_ref, known_ref, out_ref, acc_ref = refs[:slots], refs[slots], *refs[slots + 1 :]
    step = pl.program_id(0)
    own, planes = b_refs[0].shape[:2]
    size = own * planes
    rh, rl = split(jnp.concatenate([rows_of(r) for r in b_refs] + [rows_of(l_ref)], axis=0))
    here = slice(size * (slots - 1), size * slots)
    weights = jnp.concatenate([rh[here], rl[here]], axis=0)
    part = dot(jnp.concatenate([rh, rl], axis=0), weights, ((1,), (1,)))

    @pl.when(step == 0)
    def _():
        acc_ref[...] = part

    @pl.when(step > 0)
    def _():
        acc_ref[...] += part

    @pl.when(step == pl.num_programs(0) - 1)
    def _():
        n = rh.shape[0]
        full = acc_ref[...]
        full = full[:n] + full[n:]
        full = full * one_hot(full.shape, lambda r: r % planes, lambda c: c % planes)
        left = one_hot((own, full.shape[1]), lambda r: r, lambda c: (c % size) // planes)
        right = one_hot((n, n // planes), lambda r: r // planes, lambda c: c)
        new = exact(exact(left, full, ((1,), (1,))), right)
        rows = own * slots
        for copy in range(out_ref.shape[0] // rows):
            out_ref[copy * rows : (copy + 1) * rows - own, :] = known_ref[...]
            out_ref[(copy + 1) * rows - own : (copy + 1) * rows, :] = new


def gram_last(slots, later, known, copies):
    own, planes, length = slots[0].shape
    rows = own * len(slots)
    count = later.shape[0]
    lanes = 2 * GROUP
    along = lambda n: pl.BlockSpec((n, planes, lanes), lambda i: (0, 0, i))
    return pl.pallas_call(
        functools.partial(gram_last_kernel, len(slots)),
        grid=(length // lanes,),
        in_specs=[along(own)] * len(slots) + [along(count), pl.BlockSpec(known.shape, lambda i: (0, 0))],
        out_specs=pl.BlockSpec((copies * rows, rows + count), lambda i: (0, 0)),
        out_shape=jax.ShapeDtypeStruct((copies * rows, rows + count), jnp.float32),
        scratch_shapes=[pltpu.VMEM((2 * (rows + count) * planes, 2 * own * planes), jnp.float32)],
        compiler_params=pltpu.CompilerParams(vmem_limit_bytes=VMEM),
        cost_estimate=pl.CostEstimate(
            flops=4_000_000_000, bytes_accessed=4 * (rows + count) * planes * length, transcendentals=0
        ),
        name="gram_last",
    )(*slots, later, known)


def mix_kernel(band_ref, slow_ref, prod_ref, out_ref, *, cells, bands, own_rows, count, order):
    own = 2 * own_rows
    rows = bands * own
    block_rows = bands * own_rows
    planes = REACH
    band = band_ref[0]
    products = prod_ref[0, :rows, :]
    for d in range(1, prod_ref.shape[0]):
        products = products + prod_ref[d, :rows, :]
    products = products * (1.0 / cells)

    def home(r):
        turn, inside = r // own, r % own
        slot = jnp.zeros_like(r)
        for t, k in enumerate(order):
            slot = jnp.where(turn == t, k, slot)
        held = (slot + band) % bands
        return (inside // own_rows) * block_rows + held * own_rows + inside % own_rows

    place = one_hot((rows, rows), lambda r: r, home)
    last = rows - own
    flip = exact(products[last:, :last], one_hot((own, own), lambda r: r, lambda c: c), ((0,), (0,)))
    corr = jnp.concatenate(
        [jnp.concatenate([products[:last, :last], flip], axis=1), products[last:, :rows]], axis=0
    )
    corr = exact(exact(place, corr), place, ((1,), (1,)))
    eye = one_hot((rows, rows), lambda r: r, lambda c: c)
    table = jnp.concatenate([corr, eye, exact(place, products[:, rows:])], axis=1)
    tiles = [table[t : t + 8] for t in range(0, rows, 8)]
    row_id = lax.broadcasted_iota(jnp.int32, (8, 1), 0)
    for j in range(rows):
        t = j // 8
        pivot_row = tiles[t][j % 8 : j % 8 + 1]
        step = pivot_row * (1.0 / pivot_row[:, j : j + 1])
        tiles[t] = tiles[t] - jnp.where(row_id > j % 8, tiles[t][:, j : j + 1], 0.0) * step
        for u in range(t + 1, len(tiles)):
            tiles[u] = tiles[u] - tiles[u][:, j : j + 1] * step
    table = jnp.concatenate(tiles, axis=0)
    pivots = jnp.sum(table[:, :rows] * eye, axis=1, keepdims=True)
    scale = lax.rsqrt(pivots)
    scale = scale * (1.5 - 0.5 * pivots * scale * scale)
    inverse = table[:, rows : 2 * rows] * scale
    weights = table[:, 2 * rows :] * scale
    coefs = exact(weights, inverse, ((0,), (0,)))
    mine = one_hot((own, rows), lambda r: (r // own_rows) * block_rows + band * own_rows + r % own_rows, lambda c: c)
    mix = jnp.concatenate([-coefs, exact(mine, inverse)], axis=0)
    mix = exact(mix, place)
    outs = count + own
    tall = one_hot((outs * planes, outs), lambda r: r // planes, lambda c: c)
    wide = one_hot((rows, rows * planes), lambda r: r, lambda c: c // planes)
    spread = exact(exact(tall, mix), wide)
    p = lax.broadcasted_iota(jnp.int32, (8, spread.shape[1]), 0) % planes
    q = lax.broadcasted_iota(jnp.int32, (8, spread.shape[1]), 1) % planes
    pattern = jnp.zeros(p.shape, jnp.float32)
    for a in range(planes):
        for b in range(planes):
            pattern = jnp.where((p == a) & (q == b), slow_ref[a, b], pattern)
    same = (p == q).astype(jnp.float32)
    spread = spread.reshape(outs * planes // 8, 8, rows * planes)
    first = (spread * same[None]).reshape(outs * planes, rows * planes)
    second = (spread * pattern[None]).reshape(outs * planes, rows * planes)
    out_ref[...] = thrice(jnp.concatenate([first, second], axis=1))


def mix(products, band, slow_mat, cells, bands, own_rows, count, order):
    own = 2 * own_rows
    rows = bands * own
    planes = REACH
    return pl.pallas_call(
        functools.partial(mix_kernel, cells=cells, bands=bands, own_rows=own_rows, count=count, order=order),
        in_specs=[
            pl.BlockSpec(memory_space=pltpu.SMEM),
            pl.BlockSpec(memory_space=pltpu.SMEM),
            pl.BlockSpec(memory_space=pltpu.VMEM),
        ],
        out_specs=pl.BlockSpec(memory_space=pltpu.VMEM),
        out_shape=jax.ShapeDtypeStruct(((count + own) * planes, 6 * rows * planes), jnp.bfloat16),
        compiler_params=pltpu.CompilerParams(vmem_limit_bytes=VMEM),
        cost_estimate=pl.CostEstimate(flops=10_000_000_000, bytes_accessed=1 << 20, transcendentals=0),
        name="mix",
    )(band.reshape(1), slow_mat, products)


def along_y(x):
    n = len(x)
    lane = lax.broadcasted_iota(jnp.int32, (8, LANE), 1)
    zero = jnp.zeros((8, LANE), jnp.float32)
    r32 = [pltpu.roll(v, 32, 1) for v in x]
    r64 = [pltpu.roll(v, 64, 1) for v in x]
    r96 = [pltpu.roll(v, 96, 1) for v in x]
    at = lambda list_, i: list_[i] if 0 <= i < n else zero
    below32, below64, below96 = lane < 32, lane < 64, lane < 96
    out = []
    for i in range(n):
        one = jnp.where(below32, at(r32, i), at(r32, i + 1)) + jnp.where(below96, at(r96, i - 1), at(r96, i))
        two = jnp.where(below64, at(r64, i + 1), at(r64, i + 2)) + jnp.where(below64, at(r64, i - 2), at(r64, i - 1))
        three = jnp.where(below96, at(r96, i + 2), at(r96, i + 3)) + jnp.where(below32, at(r32, i - 3), at(r32, i - 2))
        four = at(x, i + 3) + at(x, i - 3)
        out.append(half_weights[1] * one + half_weights[2] * two + half_weights[3] * three + half_weights[4] * four)
    return out


def stencil_kernel(x_ref, halo_ref, m_ref, z_ref, v_ref, out_ref, flat_ref, acc_ref):
    count, planes, length = x_ref.shape
    rows = count * planes
    groups = length // GROUP
    flat_ref[...] = rows_of(x_ref)
    vectors = length // LANE

    def eight(t, _):
        at = pl.ds(pl.multiple_of(t * 8, 8), 8)
        x = [flat_ref[at, i * LANE : (i + 1) * LANE] for i in range(vectors)]
        ys = along_y(x)
        for i in range(vectors):
            acc_ref[at, i * LANE : (i + 1) * LANE] = ys[i] + v_ref[:, i * LANE : (i + 1) * LANE] * x[i]
        return 0

    lax.fori_loop(0, rows // 8, eight, 0)
    for g in range(groups):
        here = slice(g * GROUP, (g + 1) * GROUP)
        x = flat_ref[:, here]
        xh, xl = split(x)
        total = dot(jnp.concatenate([xh, xl, xh], axis=1), z_ref[...])
        total += dot(m_ref[...], stacked(jnp.concatenate([x, halo_ref[:, :, here].reshape(rows, GROUP)], axis=0)))
        total += acc_ref[:, here]
        out_ref[:, :, here] = total.reshape(count, planes, GROUP)


def stencil(x, halo, odd, potential, block):
    count, planes, length = x.shape
    size = block * planes
    within = plane_matrix(0)
    m = thrice_constant(spread_variants([(within, plane_matrix(planes)), (within, plane_matrix(-planes))], block))
    zh, zl = split_constant(z_matrix())
    z = jnp.concatenate([zh, zh, zl], axis=0)
    v = jnp.concatenate([potential, potential], axis=0)
    spec = pl.BlockSpec((block, planes, length), lambda i, odd: (i, 0, 0))
    picked = pl.BlockSpec((pl.squeezed,) + m.shape[1:], lambda i, odd: (odd[0], 0, 0))
    fixed = lambda a: pl.BlockSpec(a.shape, lambda i, odd: (0, 0))
    return pl.pallas_call(
        lambda odd_ref, *refs: stencil_kernel(*refs),
        grid_spec=pltpu.PrefetchScalarGridSpec(
            num_scalar_prefetch=1,
            grid=(count // block,),
            in_specs=[spec, spec, picked, fixed(z), fixed(v)],
            out_specs=spec,
            scratch_shapes=[pltpu.VMEM((size, length), jnp.float32)] * 2,
        ),
        out_shape=jax.ShapeDtypeStruct(x.shape, jnp.float32),
        compiler_params=pltpu.CompilerParams(vmem_limit_bytes=VMEM),
        cost_estimate=pl.CostEstimate(flops=100_000_000 * count, bytes_accessed=12 * x.size, transcendentals=0),
        name="stencil",
    )(odd, x, halo, m, z, v)


def final_kernel(slots, kind_ref, far_ref, base_ref, near_later, far_later, *refs):
    hb_refs, refs = refs[:slots], refs[slots:]
    slow_ref, near_refs, far_refs = refs[0], refs[1:slots], refs[slots : 2 * slots - 1]
    k_ref, m_ref, later_ref, block_ref = refs[2 * slots - 1 :]
    count, planes, lanes = base_ref.shape
    rows = count * planes
    is_far = far_ref[0] > 0
    pick = lambda far, near: jnp.where(is_far, far[...], near[...]).reshape(near.shape[0] * planes, lanes)
    hb = jnp.concatenate([rows_of(r) for r in hb_refs], axis=0)
    slow = jnp.concatenate([rows_of(slow_ref)] + [pick(f, n) for f, n in zip(far_refs, near_refs)], axis=0)
    total = dot(m_ref[...], stacked(jnp.concatenate([hb, slow], axis=0)))
    tall = total[:rows] + dot(k_ref[...], stacked(pick(far_later, near_later)))
    later_ref[...] = base_ref[...] + tall.reshape(count, planes, lanes)
    block_ref[...] = total[rows:].reshape(block_ref.shape)


def final(kind, is_far, base, near_later, far_later, hb, slow_mine, near_slow, far_slow, mats):
    count, planes, length = base.shape
    own = slow_mine.shape[0]
    none = np.zeros((planes, planes), np.float32)
    k = thrice_constant(spread_variants([(plane_matrix(-planes),), (plane_matrix(planes),), (none,)], count))
    lanes = 2 * GROUP
    along = lambda n: pl.BlockSpec((n, planes, lanes), lambda i, kind, far: (0, 0, i))
    near = lambda n: pl.BlockSpec((n, planes, lanes), lambda i, kind, far: (0, 0, i * (1 - far[0])))
    far = lambda n: pl.BlockSpec((n, planes, lanes), lambda i, kind, far: (0, 0, i * far[0]))
    picked = pl.BlockSpec((pl.squeezed,) + k.shape[1:], lambda i, kind, far: (kind[0], 0, 0))
    return pl.pallas_call(
        functools.partial(final_kernel, len(hb)),
        grid_spec=pltpu.PrefetchScalarGridSpec(
            num_scalar_prefetch=2,
            grid=(length // lanes,),
            in_specs=[along(count), near(count), far(count)]
            + [along(own)] * (len(hb) + 1)
            + [near(own)] * len(near_slow)
            + [far(own)] * len(far_slow)
            + [picked, pl.BlockSpec(mats.shape, lambda i, kind, far: (0, 0))],
            out_specs=[along(count), along(own)],
        ),
        out_shape=[
            jax.ShapeDtypeStruct((count, planes, length), jnp.float32),
            jax.ShapeDtypeStruct((own, planes, length), jnp.float32),
        ],
        compiler_params=pltpu.CompilerParams(vmem_limit_bytes=VMEM),
        cost_estimate=pl.CostEstimate(flops=8_000_000_000, bytes_accessed=24 * base.size, transcendentals=0),
        name="final",
    )(kind, is_far, base, near_later, far_later, *hb, slow_mine, *near_slow, *far_slow, k, mats)


def after(x, *others):
    return lax.optimization_barrier((x,) + others)[0]


def local(blocks, later, potential):
    pair, own_rows, planes, length = blocks.shape
    count = later.shape[0]
    ns, nb = lax.axis_size("space"), lax.axis_size("band")
    s, band = lax.axis_index("space"), lax.axis_index("band")
    cells = planes * ns * length
    own = pair * own_rows
    both = ("space", "band")

    fast_pairs = [(i, i ^ 1) for i in range(ns)]
    near = [(i, i + 1) for i in range(1, ns - 1, 4)]
    near += [(j, i) for i, j in near]
    across = range(3, ns - 1, 4)
    far = [(i, i + 1) for i in across] + [(i + 1, i) for i in across]
    hop_one = [(i, i + 4) for i in across] + [(i + 1, i - 3) for i in across]
    hop_two = [(i + 4, i + 1) for i in across] + [(i - 3, i) for i in across]
    is_far = ((s % 4 == 3) & (s < ns - 1)) | ((s % 4 == 0) & (s > 0))
    two = is_far.astype(jnp.int32).reshape(1)
    ring = [(b + 1, b) for b in range(nb - 1)] + [(0, nb - 1)]

    odd = (s % 2).astype(jnp.int32).reshape(1)
    edge = (s == 0) | (s == ns - 1)
    kind = jnp.where(edge, 2, odd)
    before, behind = plane_matrix(-planes), plane_matrix(planes)
    slow_mat = jnp.where(edge, 0.0, jnp.where(s % 2 == 0, before, behind))

    mine = blocks.reshape(own, planes, length)
    slots, slow = [None] * nb, [None] * nb
    slots[0] = mine
    up = lambda x: lax.ppermute(x, "band", ring)
    down = lambda x: lax.ppermute(x, "band", [(j, i) for i, j in ring])
    swap = lambda x: lax.ppermute(x, "space", fast_pairs)
    near_ring = [(i * nb + b, i * nb + c) for i, _ in near for b, c in ring]
    near_up = lambda x: lax.ppermute(x, both, near_ring)
    near_down = lambda x: lax.ppermute(x, both, [(j, i) for i, j in near_ring])
    cross = lambda x: lax.ppermute(x, "space", far)

    middle = nb // 2
    order = [0] + sorted(range(1, nb), key=lambda k: (min(k, nb - k), k))
    slots[1], slots[-1] = up(mine), down(mine)
    fast_mine, fast_later = swap(mine), swap(later)
    hop = lax.ppermute(later, "space", hop_one)
    near_later = lax.ppermute(later, "space", near)
    slow_mine = lax.ppermute(mine, "space", near + far)
    hb = [None] * nb
    hb[0] = stencil(mine, fast_mine, odd, potential, own)
    base = stencil(later, fast_later, odd, potential, min(32, count))
    slots[1], slots[-1], hop, base, hb[0] = lax.optimization_barrier((slots[1], slots[-1], hop, base, hb[0]))
    for k in order[1:]:
        if slots[k] is None:
            slots[k] = up(slots[k - 1]) if k <= middle else down(slots[k + 1])
    far_later = lax.ppermute(hop, "space", hop_two)
    fast = {k: swap(slots[k]) for k in order[1:-1]}
    far_slow = {k: cross(slots[k]) for k in order[1:-1]}
    for k in order[1:-1]:
        hb[k] = stencil(slots[k], fast[k], odd, potential, own)
    known = gram([slots[k] for k in order[:-1]], after(later, *fast.values()))
    slots[middle], known, slow_mine, *rest = lax.optimization_barrier(
        (slots[middle], known, slow_mine, *[hb[k] for k in order[:-1]])
    )
    for k, h in zip(order[:-1], rest):
        hb[k] = h
    near_slow = {0: slow_mine}
    for k in order[1:-1]:
        near_slow[k] = near_up(near_slow[k - 1]) if k < middle else near_down(near_slow[(k + 1) % nb])
    far_slow[middle] = cross(slots[middle])
    copies = 4
    products = lax.all_gather(gram_last([slots[k] for k in order], later, known, copies), "space")
    hb[middle] = stencil(slots[middle], swap(slots[middle]), odd, potential, own)
    near_slow[middle] = near_up(near_slow[middle - 1])
    mats = mix(products, band, slow_mat, cells, nb, own_rows, count, order)
    pick = lambda d: [d[k] for k in order[1:]]
    h_later, h_block = final(
        kind, two, base, near_later, far_later, [hb[k] for k in order], slow_mine, pick(near_slow), pick(far_slow), mats
    )
    return h_block.reshape(blocks.shape), h_later


def solution(mesh):
    return jax.shard_map(
        local,
        mesh=mesh,
        in_specs=(P(None, "band", "space", None), P("band", "space", None), P("space", None)),
        out_specs=(P(None, "band", "space", None), P("band", "space", None)),
        check_vma=False,
    )
```

time: 254 us -> 215 us (0.85)
  waiting for transfers between devices: 103 us -> 50.2 us
  local copies, waits for them, and re-layouts: 17.1 us -> 1.16 us
  between operations: 1.1 us -> 14.2 us
  Pallas kernels: 91.3 us -> 104 us
  starting transfers between devices: 32.7 us -> 39.9 us
    ppermute x9 -> x10, waiting for transfers between devices: 80.3 us -> 16.6 us  [the longest x2 12 us: local(): near_up = lambda x: lax.ppermute(x, both, near_ring)]
    unnamed x74 -> x16, local copies, waits for them, and re-layouts: 17.1 us -> 1.16 us
    ppermute x2, waiting for transfers between devices: 16.1 us -> 28.2 us  [local(): up = lambda x: lax.ppermute(x, 'band', ring)]
    pallas_call x5, Pallas kernels: 49.6 us -> 56.1 us  [stencil(): pl.pallas_call(lambda odd_ref, *refs: stencil_kernel(*refs), grid_spec=pl...]
    ppermute x9 -> x10, starting transfers between devices: 24.4 us -> 29.9 us  [the longest x2 12.7 us: local(): near_up = lambda x: lax.ppermute(x, both, near_ring)]
    pallas_call x2, Pallas kernels: 22 us -> 27.4 us  [the longest x1 17 us: final(): pl.pallas_call(functools.partial(final_kernel, len(hb)), grid_spec=pltpu....]
    select_n x2 -> x0, other arithmetic: 3.41 us -> none  [local(): jnp.where(is_far, slots[k], slow[k - 1] if low else slow[(k + 1) % nb])]
    ppermute x5, starting transfers between devices: 1.09 us -> 3.8 us  [local(): swap = lambda x: lax.ppermute(x, 'space', fast_pairs)]
  transfers between devices with their start and end apart: 17 -> 19, of which waited for: 7 -> 5; matrix products, arithmetic and copies ran while one was open for 2% -> 1% of each run, Pallas kernels for 32% -> 41%
where the time goes in v1:
time: 215 us; the launch traced here: 212 us
  Pallas kernels  104 us (48%)
  waiting for transfers between devices  50.2 us (23%)
  starting transfers between devices  39.9 us (19%)
  between operations  14.2 us (7%)
  other arithmetic  2.27 us (1%)
    pallas_call x5, Pallas kernels, stencil(): pl.pallas_call(lambda odd_ref, *refs: stencil_kernel(*refs), grid_spec=pl...  56.1 us
    ppermute x2, waiting for transfers between devices, local(): up = lambda x: lax.ppermute(x, 'band', ring)  28.2 us
    pallas_call x1, Pallas kernels, final(): pl.pallas_call(functools.partial(final_kernel, len(hb)), grid_spec=pltpu....  17 us
    ppermute x2, starting transfers between devices, local(): near_up = lambda x: lax.ppermute(x, both, near_ring)  12.7 us
    ppermute x2, waiting for transfers between devices, local(): near_up = lambda x: lax.ppermute(x, both, near_ring)  12 us
    pallas_call x1, Pallas kernels, gram(): pl.pallas_call(functools.partial(gram_kernel, len(slots)), grid=(length /...  10.9 us
    pallas_call x1, Pallas kernels, gram_last(): pl.pallas_call(functools.partial(gram_last_kernel, len(slots)), grid=(len...  10.4 us
    pallas_call x1, Pallas kernels, mix(): pl.pallas_call(functools.partial(mix_kernel, cells=cells, bands=bands, ow...  9.57 us
  transfers between devices with their start and end apart: 19, of which 5 were waited for; matrix products, arithmetic and copies ran while one was open for 1% of the time, Pallas kernels for 41%

profile of v1, /device:TPU:6, one launch (start us, length us, event | category | flops | bytes accessed | tf_op | source)
XLA Modules:
  0.0 211.8 jit_solution(13061881670061955518)
XLA Ops:
  7.2 0.1 collective-permute-start.3
  7.3 3.3 %collective-permute-start.2 = (f32[64,4,6144]{2,1,0:T(4,128)}, f32[64,4,6144]{2,1,0:T(4,128)}, u32[]{:S(2)}, u32[]{:S(2)}) collective-permute-start(f32[64,4,6144]{2,1,0:T(4,128)} %refs_4_.1), channel_id=1, source_target_pairs={{12,28},{16,0},{13,29},{17,1},{14,30},{18,2},{15,31},{19,3}} | collective-permute-start | bytes 18874376 | tf_op jit(solution)/shard_map/ppermute | solution.py:449
  10.6 1.6 collective-permute-start.1
  12.2 2.2 %collective-permute-start = (f32[16,4,6144]{2,1,0:T(4,128)}, f32[16,4,6144]{2,1,0:T(4,128)}, u32[]{:S(2)}, u32[]{:S(2)}) collective-permute-start(f32[16,4,6144]{2,1,0:T(4,128)} %bitcast.3.refs_0_), channel_id=1, source_target_pairs={{1,0},{2,1},{3,2},{0,3},{5,4},{6,5},{7,6},{4,7},{9,8},{10,9},{11,1... | collective-permute-start | bytes 4718600 | tf_op jit(solution)/shard_map/ppermute | solution.py:437
  14.4 5.5 %collective-permute-done.4.refs_1_ = f32[16,4,6144]{2,1,0:T(4,128)S(1)} collective-permute-done((f32[16,4,6144]{2,1,0:T(4,128)}, f32[16,4,6144]{2,1,0:T(4,128)S(1)}, u32[]{:S(2)}, u32[]{:S(2)}) %collective-permute-start.4) | collective-permute-done | bytes 1572896 | tf_op jit(solution)/shard_map/ppermute | solution.py:439
  19.9 2.2 %collective-permute-start.5 = (f32[64,4,6144]{2,1,0:T(4,128)}, f32[64,4,6144]{2,1,0:T(4,128)}, u32[]{:S(2)}, u32[]{:S(2)}) collective-permute-start(f32[64,4,6144]{2,1,0:T(4,128)} %refs_4_.1), channel_id=1, source_target_pairs={{4,8},{20,24},{8,4},{24,20},{5,9},{21,25},{9,5},{25,21},{6,10},{22... | collective-permute-start | bytes 18874376 | tf_op jit(solution)/shard_map/ppermute | solution.py:450
  22.1 1.7 pad_maximum_fusion.refs_4_
  23.8 8.4 %stencil.6.refs_0_ = f32[16,4,6144]{2,1,0:T(4,128)} custom-call(s32[1]{0:T(128)} %bitcast.1.odd_ref, f32[16,4,6144]{2,1,0:T(4,128)} %bitcast.3.refs_0_, f32[16,4,6144]{2,1,0:T(4,128)} %copy-done.5, bf16[2,64,384]{2,1,0:T(8,128)(2,1)} %constant.60.clone.refs_2_, bf16[1152,384]{1,0:T(8,128)(2,1)} %constant.68.refs_3_, f32[8,6144]{1,0:T(8,128)} %pad_maximum_fusion.refs_4_), custom_call_target="tpu_custom_call" | custom-call | flops 1600000000 | bytes 4718592 | tf_op jit(solution)/shard_map/stencil/pallas_call | solution.py:340
  32.2 22.3 %stencil.5.base_ref = f32[64,4,6144]{2,1,0:T(4,128)} custom-call(s32[1]{0:T(128)} %bitcast.1.odd_ref, f32[64,4,6144]{2,1,0:T(4,128)} %refs_4_.1, f32[64,4,6144]{2,1,0:T(4,128)} %collective-permute-done.3.refs_1_, bf16[2,128,768]{2,1,0:T(8,128)(2,1)} %constant.63.clone.refs_2_, bf16[1152,384]{1,0:T(8,128)(2,1)} %constant.68.refs_3_, ...), custom_call_target="tpu_custom_call" | custom-call | flops 6400000000 | bytes 18874368 | tf_op jit(solution)/shard_map/stencil/pallas_call | solution.py:340
  54.6 28.2 %collective-permute-done.refs_1_.refs_0_ = f32[16,4,6144]{2,1,0:T(4,128)} collective-permute-done((f32[16,4,6144]{2,1,0:T(4,128)}, f32[16,4,6144]{2,1,0:T(4,128)}, u32[]{:S(2)}, u32[]{:S(2)}) %collective-permute-start) | collective-permute-done | bytes 1572896 | tf_op jit(solution)/shard_map/ppermute | solution.py:437
  82.7 3.3 %collective-permute-start.6 = (f32[64,4,6144]{2,1,0:T(4,128)}, f32[64,4,6144]{2,1,0:T(4,128)}, u32[]{:S(2)}, u32[]{:S(2)}) collective-permute-start(f32[64,4,6144]{2,1,0:T(4,128)} %collective-permute-done.2), channel_id=1, source_target_pairs={{28,16},{0,12},{29,17},{1,13},{30,18},{2,14},{31,19},{3,15}} | collective-permute-start | bytes 18874376 | tf_op jit(solution)/shard_map/ppermute | solution.py:459
  86.0 3.6 %collective-permute-start.8 = (f32[16,4,6144]{2,1,0:T(4,128)}, f32[16,4,6144]{2,1,0:T(4,128)S(1)}, u32[]{:S(2)}, u32[]{:S(2)}) collective-permute-start(f32[16,4,6144]{2,1,0:T(4,128)} %collective-permute-done.refs_1_.refs_0_), channel_id=1, source_target_pairs={{0,4},{4,0},{8,12},{12,8},{16,20},{20,16},{24,28},{28,24},{1,5},{5... | collective-permute-start | bytes 4718600 | tf_op jit(solution)/shard_map/ppermute | solution.py:439
  89.7 1.9 collective-permute-start.10
  91.6 2.3 %collective-permute-start.7 = (f32[16,4,6144]{2,1,0:T(4,128)}, f32[16,4,6144]{2,1,0:T(4,128)}, u32[]{:S(2)}, u32[]{:S(2)}) collective-permute-start(f32[16,4,6144]{2,1,0:T(4,128)} %collective-permute-done.refs_1_.refs_0_), channel_id=1, source_target_pairs={{1,0},{2,1},{3,2},{0,3},{5,4},{6,5},{7,6},{4,7},{9,8},{10,9},{11,1... | collective-permute-start | bytes 4718600 | tf_op jit(solution)/shard_map/ppermute | solution.py:437
  94.0 1.1 copy-done.7
  95.1 0.9 collective-permute-start.16
  96.1 8.5 %stencil.8.refs_2_ = f32[16,4,6144]{2,1,0:T(4,128)} custom-call(s32[1]{0:T(128)} %bitcast.1.odd_ref, f32[16,4,6144]{2,1,0:T(4,128)} %copy-done.4, f32[16,4,6144]{2,1,0:T(4,128)} %copy-done.6, bf16[2,64,384]{2,1,0:T(8,128)(2,1)} %constant.60.clone.refs_2_, bf16[1152,384]{1,0:T(8,128)(2,1)} %constant.68.refs_3_, f32[8,6144]{1,0:T(8,128)} %pad_maximum_fusion.refs_4_), custom_call_target="tpu_custom_call" | custom-call | flops 1600000000 | bytes 4718592 | tf_op jit(solution)/shard_map/stencil/pallas_call | solution.py:340
  104.6 8.4 %stencil.7.refs_1_ = f32[16,4,6144]{2,1,0:T(4,128)} custom-call(s32[1]{0:T(128)} %bitcast.1.odd_ref, f32[16,4,6144]{2,1,0:T(4,128)} %collective-permute-done.refs_1_.refs_0_, f32[16,4,6144]{2,1,0:T(4,128)} %copy-done.7, bf16[2,64,384]{2,1,0:T(8,128)(2,1)} %constant.60.clone.refs_2_, bf16[1152,384]{1,0:T(8,128)(2,1)} %constant.68.refs_3_, ...), custom_call_target="tpu_custom_call" | custom-call | flops 1600000000 | bytes 4718592 | tf_op jit(solution)/shard_map/stencil/pallas_call | solution.py:340
  112.9 10.9 %gram.1.refs_5_ = f32[48,128]{1,0:T(8,128)} custom-call(f32[16,4,6144]{2,1,0:T(4,128)} %bitcast.3.refs_0_, f32[16,4,6144]{2,1,0:T(4,128)} %collective-permute-done.refs_1_.refs_0_, f32[16,4,6144]{2,1,0:T(4,128)} %copy-done.4, f32[64,4,6144]{2,1,0:T(4,128)} %refs_4_.1), custom_call_target="tpu_custom_call" | custom-call | flops 8000000000 | bytes 11010048 | tf_op jit(solution)/shard_map/gram/pallas_call | solution.py:132
  123.8 4.6 %collective-permute-done.10.refs_4_ = f32[16,4,6144]{2,1,0:T(4,128)S(1)} collective-permute-done((f32[16,4,6144]{2,1,0:T(4,128)}, f32[16,4,6144]{2,1,0:T(4,128)S(1)}, u32[]{:S(2)}, u32[]{:S(2)}) %collective-permute-start.10) | collective-permute-done | bytes 1572896 | tf_op jit(solution)/shard_map/ppermute | solution.py:451
  128.4 6.0 %collective-permute-start.12 = (f32[16,4,6144]{2,1,0:T(4,128)S(1)}, f32[16,4,6144]{2,1,0:T(4,128)}, u32[]{:S(2)}, u32[]{:S(2)}) collective-permute-start(f32[16,4,6144]{2,1,0:T(4,128)S(1)} %collective-permute-done.10.refs_4_), channel_id=1, source_target_pairs={{5,4},{6,5},{7,6},{4,7},{21,20},{22,21},{23,22},{20,23},{9,8},{10,... | collective-permute-start | bytes 4718600 | tf_op jit(solution)/shard_map/ppermute | solution.py:441
  134.5 10.4 %gram_last.1 = f32[256,128]{1,0:T(8,128)} custom-call(f32[16,4,6144]{2,1,0:T(4,128)} %bitcast.3.refs_0_, f32[16,4,6144]{2,1,0:T(4,128)} %collective-permute-done.refs_1_.refs_0_, f32[16,4,6144]{2,1,0:T(4,128)} %copy-done.4, f32[16,4,6144]{2,1,0:T(4,128)} %collective-permute-done.7.refs_0_.refs_3_, f32[64,4,6144]{2,1,0:T(4,128)} %refs_4_.1, ...), custom_call_target="tpu_custom_call" | custom-call | flops 4000000000 | bytes 12582912 | tf_op jit(solution)/shard_map/gram_last/pallas_call | solution.py:186
  145.0 1.8 collective-permute-start.15
  146.8 1.9 collective-permute-start.13
  148.8 3.7 %collective-permute-done.12.refs_5_ = f32[16,4,6144]{2,1,0:T(4,128)} collective-permute-done((f32[16,4,6144]{2,1,0:T(4,128)S(1)}, f32[16,4,6144]{2,1,0:T(4,128)}, u32[]{:S(2)}, u32[]{:S(2)}) %collective-permute-start.12) | collective-permute-done | bytes 1572896 | tf_op jit(solution)/shard_map/ppermute | solution.py:441
  152.4 1.9 collective-permute-start.17
  154.3 6.6 %collective-permute-start.14 = (f32[16,4,6144]{2,1,0:T(4,128)}, f32[16,4,6144]{2,1,0:T(4,128)}, u32[]{:S(2)}, u32[]{:S(2)}) collective-permute-start(f32[16,4,6144]{2,1,0:T(4,128)} %collective-permute-done.12.refs_5_), channel_id=1, source_target_pairs={{5,4},{6,5},{7,6},{4,7},{21,20},{22,21},{23,22},{20,23},{9,8},{10,... | collective-permute-start | bytes 4718600 | tf_op jit(solution)/shard_map/ppermute | solution.py:441
  161.0 0.6 select_select_fusion.slow_ref
  161.6 8.5 %stencil.9.refs_3_ = f32[16,4,6144]{2,1,0:T(4,128)} custom-call(s32[1]{0:T(128)} %bitcast.1.odd_ref, f32[16,4,6144]{2,1,0:T(4,128)} %collective-permute-done.7.refs_0_.refs_3_, f32[16,4,6144]{2,1,0:T(4,128)} %collective-permute-done.11.refs_1_, bf16[2,64,384]{2,1,0:T(8,128)(2,1)} %constant.60.clone.refs_2_, bf16[1152,384]{1,0:T(8,128)(2,1)} %constant.68.refs_3_, ...), custom_call_target="tpu_custom_call" | custom-call | flops 1600000000 | bytes 4718592 | tf_op jit(solution)/shard_map/stencil/pallas_call | solution.py:340
  170.0 9.6 %mix.1.refs_12_ = bf16[320,1536]{1,0:T(8,128)(2,1)} custom-call(s32[1]{0:T(128)} %bitcast.4.band_ref, f32[4,4]{1,0:T(4,128)} %select_select_fusion.slow_ref, f32[8,256,128]{2,1,0:T(8,128)} %bitcast.8), custom_call_target="tpu_custom_call" | custom-call | flops 10000000000 | bytes 1048576 | tf_op jit(solution)/shard_map/mix/pallas_call | solution.py:269
  179.6 8.3 %collective-permute-done.14.refs_7_ = f32[16,4,6144]{2,1,0:T(4,128)} collective-permute-done((f32[16,4,6144]{2,1,0:T(4,128)}, f32[16,4,6144]{2,1,0:T(4,128)}, u32[]{:S(2)}, u32[]{:S(2)}) %collective-permute-start.14) | collective-permute-done | bytes 1572896 | tf_op jit(solution)/shard_map/ppermute | solution.py:441
  187.9 17.0 %final.1 = (f32[64,4,6144]{2,1,0:T(4,128)}, f32[16,4,6144]{2,1,0:T(4,128)}) custom-call(s32[1]{0:T(128)S(6)} %select_n.41.kind_ref, s32[1]{0:T(128)} %bitcast.2.far_ref, f32[64,4,6144]{2,1,0:T(4,128)} %stencil.5.base_ref, f32[64,4,6144]{2,1,0:T(4,128)} %collective-permute-done.5.near_later, f32[64,4,6144]{2,1,0:T(4,128)} %collective-permute-done.6.far_later, ...), custom_call_target="tpu_custom_call" | custom-call | flops 8000000000 | bytes 37748736 | tf_op jit(solution)/shard_map/final/pallas_call | solution.py:382
  (34 shorter events, 0.2 us)
Async XLA Ops:
  7.2 162.9 %all-gather.3.cloned.1.call-start = ((), (), s32[]{:S(2)}) async-start(), calls=%async_computation | async-start | bytes 1179648 | tf_op jit(solution)/shard_map/all_gather | solution.py:475
  7.2 25.0 %collective-permute-start.3 = (f32[64,4,6144]{2,1,0:T(4,128)}, f32[64,4,6144]{2,1,0:T(4,128)}, u32[]{:S(2)}, u32[]{:S(2)}) collective-permute-start(f32[64,4,6144]{2,1,0:T(4,128)} %refs_4_.1), channel_id=1, source_target_pairs={{0,4},{4,0},{8,12},{12,8},{16,20},{20,16},{24,28},{28,24},{1,5},{5... | collective-permute-start | bytes 18874376 | tf_op jit(solution)/shard_map/ppermute | solution.py:439
  7.3 75.4 %collective-permute-start.2 = (f32[64,4,6144]{2,1,0:T(4,128)}, f32[64,4,6144]{2,1,0:T(4,128)}, u32[]{:S(2)}, u32[]{:S(2)}) collective-permute-start(f32[64,4,6144]{2,1,0:T(4,128)} %refs_4_.1), channel_id=1, source_target_pairs={{12,28},{16,0},{13,29},{17,1},{14,30},{18,2},{15,31},{19,3}} | collective-permute-start | bytes 18874376 | tf_op jit(solution)/shard_map/ppermute | solution.py:449
  10.6 9.3 %collective-permute-start.4 = (f32[16,4,6144]{2,1,0:T(4,128)}, f32[16,4,6144]{2,1,0:T(4,128)S(1)}, u32[]{:S(2)}, u32[]{:S(2)}) collective-permute-start(f32[16,4,6144]{2,1,0:T(4,128)} %bitcast.3.refs_0_), channel_id=1, source_target_pairs={{0,4},{4,0},{8,12},{12,8},{16,20},{20,16},{24,28},{28,24},{1,5},{5... | collective-permute-start | bytes 4718600 | tf_op jit(solution)/shard_map/ppermute | solution.py:439
  10.6 44.0 %collective-permute-start.1 = (f32[16,4,6144]{2,1,0:T(4,128)}, f32[16,4,6144]{2,1,0:T(4,128)S(1)}, u32[]{:S(2)}, u32[]{:S(2)}) collective-permute-start(f32[16,4,6144]{2,1,0:T(4,128)} %bitcast.3.refs_0_), channel_id=1, source_target_pairs={{0,1},{1,2},{2,3},{3,0},{4,5},{5,6},{6,7},{7,4},{8,9},{9,10},{10,1... | collective-permute-start | bytes 4718600 | tf_op jit(solution)/shard_map/ppermute | solution.py:438
  12.2 70.5 %collective-permute-start = (f32[16,4,6144]{2,1,0:T(4,128)}, f32[16,4,6144]{2,1,0:T(4,128)}, u32[]{:S(2)}, u32[]{:S(2)}) collective-permute-start(f32[16,4,6144]{2,1,0:T(4,128)} %bitcast.3.refs_0_), channel_id=1, source_target_pairs={{1,0},{2,1},{3,2},{0,3},{5,4},{6,5},{7,6},{4,7},{9,8},{10,9},{11,1... | collective-permute-start | bytes 4718600 | tf_op jit(solution)/shard_map/ppermute | solution.py:437
  19.9 3.9 %copy-start.5 = (f32[16,4,6144]{2,1,0:T(4,128)}, f32[16,4,6144]{2,1,0:T(4,128)S(1)}, u32[]{:S(2)}) copy-start(f32[16,4,6144]{2,1,0:T(4,128)S(1)} %collective-permute-done.4.refs_1_) | copy-start | bytes 4718596
  19.9 125.1 %collective-permute-start.5 = (f32[64,4,6144]{2,1,0:T(4,128)}, f32[64,4,6144]{2,1,0:T(4,128)}, u32[]{:S(2)}, u32[]{:S(2)}) collective-permute-start(f32[64,4,6144]{2,1,0:T(4,128)} %refs_4_.1), channel_id=1, source_target_pairs={{4,8},{20,24},{8,4},{24,20},{5,9},{21,25},{9,5},{25,21},{6,10},{22... | collective-permute-start | bytes 18874376 | tf_op jit(solution)/shard_map/ppermute | solution.py:450
  54.6 39.4 %copy-start.4 = (f32[16,4,6144]{2,1,0:T(4,128)}, f32[16,4,6144]{2,1,0:T(4,128)S(1)}, u32[]{:S(2)}) copy-start(f32[16,4,6144]{2,1,0:T(4,128)S(1)} %collective-permute-done.1.refs_2_.refs_0_) | copy-start | bytes 4718596
  82.7 8.9 %collective-permute-start.9 = (f32[16,4,6144]{2,1,0:T(4,128)S(1)}, f32[16,4,6144]{2,1,0:T(4,128)S(1)}, u32[]{:S(2)}, u32[]{:S(2)}) collective-permute-start(f32[16,4,6144]{2,1,0:T(4,128)S(1)} %collective-permute-done.1.refs_2_.refs_0_), channel_id=1, source_target_pairs={{0,4},{4,0},{8,12},{12,8},{16,20},{20,16},{24,28},{28,24},{1,5},{5... | collective-permute-start | bytes 4718600 | tf_op jit(solution)/shard_map/ppermute | solution.py:439
  82.7 105.2 %collective-permute-start.6 = (f32[64,4,6144]{2,1,0:T(4,128)}, f32[64,4,6144]{2,1,0:T(4,128)}, u32[]{:S(2)}, u32[]{:S(2)}) collective-permute-start(f32[64,4,6144]{2,1,0:T(4,128)} %collective-permute-done.2), channel_id=1, source_target_pairs={{28,16},{0,12},{29,17},{1,13},{30,18},{2,14},{31,19},{3,15}} | collective-permute-start | bytes 18874376 | tf_op jit(solution)/shard_map/ppermute | solution.py:459
  86.0 7.9 %collective-permute-start.8 = (f32[16,4,6144]{2,1,0:T(4,128)}, f32[16,4,6144]{2,1,0:T(4,128)S(1)}, u32[]{:S(2)}, u32[]{:S(2)}) collective-permute-start(f32[16,4,6144]{2,1,0:T(4,128)} %collective-permute-done.refs_1_.refs_0_), channel_id=1, source_target_pairs={{0,4},{4,0},{8,12},{12,8},{16,20},{20,16},{24,28},{28,24},{1,5},{5... | collective-permute-start | bytes 4718600 | tf_op jit(solution)/shard_map/ppermute | solution.py:439
  89.7 38.7 %collective-permute-start.10 = (f32[16,4,6144]{2,1,0:T(4,128)}, f32[16,4,6144]{2,1,0:T(4,128)S(1)}, u32[]{:S(2)}, u32[]{:S(2)}) collective-permute-start(f32[16,4,6144]{2,1,0:T(4,128)} %bitcast.3.refs_0_), channel_id=1, source_target_pairs={{4,8},{20,24},{8,4},{24,20},{12,16},{16,12},{5,9},{21,25},{9,5},{2... | collective-permute-start | bytes 4718600 | tf_op jit(solution)/shard_map/ppermute | solution.py:451
  91.6 2.4 %copy-start.6 = (f32[16,4,6144]{2,1,0:T(4,128)}, f32[16,4,6144]{2,1,0:T(4,128)S(1)}, u32[]{:S(2)}) copy-start(f32[16,4,6144]{2,1,0:T(4,128)S(1)} %collective-permute-done.9.refs_1_) | copy-start | bytes 4718596
  91.6 36.8 %collective-permute-start.7 = (f32[16,4,6144]{2,1,0:T(4,128)}, f32[16,4,6144]{2,1,0:T(4,128)}, u32[]{:S(2)}, u32[]{:S(2)}) collective-permute-start(f32[16,4,6144]{2,1,0:T(4,128)} %collective-permute-done.refs_1_.refs_0_), channel_id=1, source_target_pairs={{1,0},{2,1},{3,2},{0,3},{5,4},{6,5},{7,6},{4,7},{9,8},{10,9},{11,1... | collective-permute-start | bytes 4718600 | tf_op jit(solution)/shard_map/ppermute | solution.py:437
  94.0 1.1 copy-start.7
  95.1 51.7 %collective-permute-start.16 = (f32[16,4,6144]{2,1,0:T(4,128)}, f32[16,4,6144]{2,1,0:T(4,128)S(1)}, u32[]{:S(2)}, u32[]{:S(2)}) collective-permute-start(f32[16,4,6144]{2,1,0:T(4,128)} %copy-done.4), channel_id=1, source_target_pairs={{12,16},{16,12},{13,17},{17,13},{14,18},{18,14},{15,19},{19,15}} | collective-permute-start | bytes 4718600 | tf_op jit(solution)/shard_map/ppermute | solution.py:443
  123.8 37.1 %copy-start.2 = (f32[4,4]{1,0:T(4,128)S(1)}, f32[4,4]{1,0:T(4,128)}, u32[]{:S(2)}) copy-start(f32[4,4]{1,0:T(4,128)} %constant.59.clone) | copy-start | bytes 196
  123.8 37.1 %copy-start.3 = (f32[4,4]{1,0:T(4,128)S(1)}, f32[4,4]{1,0:T(4,128)}, u32[]{:S(2)}) copy-start(f32[4,4]{1,0:T(4,128)} %constant.58.clone) | copy-start | bytes 196
  128.4 18.4 %copy-start = (f32[16,4,6144]{2,1,0:T(4,128)}, f32[16,4,6144]{2,1,0:T(4,128)S(1)}, u32[]{:S(2)}) copy-start(f32[16,4,6144]{2,1,0:T(4,128)S(1)} %collective-permute-done.10.refs_4_) | copy-start | bytes 4718596
  128.4 24.0 %collective-permute-start.12 = (f32[16,4,6144]{2,1,0:T(4,128)S(1)}, f32[16,4,6144]{2,1,0:T(4,128)}, u32[]{:S(2)}, u32[]{:S(2)}) collective-permute-start(f32[16,4,6144]{2,1,0:T(4,128)S(1)} %collective-permute-done.10.refs_4_), channel_id=1, source_target_pairs={{5,4},{6,5},{7,6},{4,7},{21,20},{22,21},{23,22},{20,23},{9,8},{10,... | collective-permute-start | bytes 4718600 | tf_op jit(solution)/shard_map/ppermute | solution.py:441
  134.5 19.8 %collective-permute-start.11 = (f32[16,4,6144]{2,1,0:T(4,128)}, f32[16,4,6144]{2,1,0:T(4,128)}, u32[]{:S(2)}, u32[]{:S(2)}) collective-permute-start(f32[16,4,6144]{2,1,0:T(4,128)} %collective-permute-done.7.refs_0_.refs_3_), channel_id=1, source_target_pairs={{0,4},{4,0},{8,12},{12,8},{16,20},{20,16},{24,28},{28,24},{1,5},{5... | collective-permute-start | bytes 4718600 | tf_op jit(solution)/shard_map/ppermute | solution.py:439
  145.0 34.6 %collective-permute-start.15 = (f32[16,4,6144]{2,1,0:T(4,128)}, f32[16,4,6144]{2,1,0:T(4,128)}, u32[]{:S(2)}, u32[]{:S(2)}) collective-permute-start(f32[16,4,6144]{2,1,0:T(4,128)} %collective-permute-done.refs_1_.refs_0_), channel_id=1, source_target_pairs={{12,16},{16,12},{13,17},{17,13},{14,18},{18,14},{15,19},{19,15}} | collective-permute-start | bytes 4718600 | tf_op jit(solution)/shard_map/ppermute | solution.py:443
  146.8 23.2 %copy-start.1 = (f32[16,4,6144]{2,1,0:T(4,128)}, f32[16,4,6144]{2,1,0:T(4,128)S(1)}, u32[]{:S(2)}) copy-start(f32[16,4,6144]{2,1,0:T(4,128)S(1)} %collective-permute-done.16.refs_9_) | copy-start | bytes 4718596
  146.8 32.8 %collective-permute-start.13 = (f32[16,4,6144]{2,1,0:T(4,128)S(1)}, f32[16,4,6144]{2,1,0:T(4,128)}, u32[]{:S(2)}, u32[]{:S(2)}) collective-permute-start(f32[16,4,6144]{2,1,0:T(4,128)S(1)} %collective-permute-done.10.refs_4_), channel_id=1, source_target_pairs={{4,5},{5,6},{6,7},{7,4},{20,21},{21,22},{22,23},{23,20},{8,9},{9,1... | collective-permute-start | bytes 4718600 | tf_op jit(solution)/shard_map/ppermute | solution.py:442
  152.4 27.2 %collective-permute-start.17 = (f32[16,4,6144]{2,1,0:T(4,128)}, f32[16,4,6144]{2,1,0:T(4,128)}, u32[]{:S(2)}, u32[]{:S(2)}) collective-permute-start(f32[16,4,6144]{2,1,0:T(4,128)} %collective-permute-done.7.refs_0_.refs_3_), channel_id=1, source_target_pairs={{12,16},{16,12},{13,17},{17,13},{14,18},{18,14},{15,19},{19,15}} | collective-permute-start | bytes 4718600 | tf_op jit(solution)/shard_map/ppermute | solution.py:443
  154.3 33.6 %collective-permute-start.14 = (f32[16,4,6144]{2,1,0:T(4,128)}, f32[16,4,6144]{2,1,0:T(4,128)}, u32[]{:S(2)}, u32[]{:S(2)}) collective-permute-start(f32[16,4,6144]{2,1,0:T(4,128)} %collective-permute-done.12.refs_5_), channel_id=1, source_target_pairs={{5,4},{6,5},{7,6},{4,7},{21,20},{22,21},{23,22},{20,23},{9,8},{10,... | collective-permute-start | bytes 4718600 | tf_op jit(solution)/shard_map/ppermute | solution.py:441
Sparse Core Ops, SparseCore 0:
  145.1 23.6 all-gather.2

commit v2 on v1

--- a/solution.py
+++ b/solution.py
@@ -11,7 +11,7 @@
 NZ = 96
 REACH = 4
 LANE = 128
-VMEM = 60 << 20
+VMEM = 28 << 20
 
 stencil_weights = (-205.0 / 72.0, 8.0 / 5.0, -1.0 / 5.0, 8.0 / 315.0, -1.0 / 560.0)
 half_weights = tuple(-0.5 * w for w in stencil_weights)
@@ -281,49 +281,43 @@
     )(band.reshape(1), slow_mat, products)
 
 
-def along_y(x):
-    n = len(x)
-    lane = lax.broadcasted_iota(jnp.int32, (8, LANE), 1)
-    zero = jnp.zeros((8, LANE), jnp.float32)
-    r32 = [pltpu.roll(v, 32, 1) for v in x]
-    r64 = [pltpu.roll(v, 64, 1) for v in x]
-    r96 = [pltpu.roll(v, 96, 1) for v in x]
-    at = lambda list_, i: list_[i] if 0 <= i < n else zero
-    below32, below64, below96 = lane < 32, lane < 64, lane < 96
-    out = []
-    for i in range(n):
-        one = jnp.where(below32, at(r32, i), at(r32, i + 1)) + jnp.where(below96, at(r96, i - 1), at(r96, i))
-        two = jnp.where(below64, at(r64, i + 1), at(r64, i + 2)) + jnp.where(below64, at(r64, i - 2), at(r64, i - 1))
-        three = jnp.where(below96, at(r96, i + 2), at(r96, i + 3)) + jnp.where(below32, at(r32, i - 3), at(r32, i - 2))
-        four = at(x, i + 3) + at(x, i - 3)
-        out.append(half_weights[1] * one + half_weights[2] * two + half_weights[3] * three + half_weights[4] * four)
-    return out
-
-
-def stencil_kernel(x_ref, halo_ref, m_ref, z_ref, v_ref, out_ref, flat_ref, acc_ref):
+def along_y(vector, n, i, cache):
+    rows = vector(i).shape[0]
+    lane = lax.broadcasted_iota(jnp.int32, (rows, LANE), 1)
+
+    def rolled(j, shift):
+        if not 0 <= j < n:
+            return jnp.zeros((rows, LANE), jnp.float32)
+        if shift and (j, shift) not in cache:
+            cache[j, shift] = pltpu.roll(vector(j), shift, 1)
+        return cache[j, shift] if shift else vector(j)
+
+    def joined(edge, j, k, shift):
+        return jnp.where(lane < edge, rolled(j, shift), rolled(k, shift))
+
+    one = joined(32, i, i + 1, 32) + joined(96, i - 1, i, 96)
+    two = joined(64, i + 1, i + 2, 64) + joined(64, i - 2, i - 1, 64)
+    three = joined(96, i + 2, i + 3, 96) + joined(32, i - 3, i - 2, 32)
+    four = rolled(i + 3, 0) + rolled(i - 3, 0)
+    return half_weights[1] * one + half_weights[2] * two + half_weights[3] * three + half_weights[4] * four
+
+
+def stencil_kernel(x_ref, halo_ref, m_ref, z_ref, v_ref, out_ref):
     count, planes, length = x_ref.shape
     rows = count * planes
-    groups = length // GROUP
-    flat_ref[...] = rows_of(x_ref)
-    vectors = length // LANE
-
-    def eight(t, _):
-        at = pl.ds(pl.multiple_of(t * 8, 8), 8)
-        x = [flat_ref[at, i * LANE : (i + 1) * LANE] for i in range(vectors)]
-        ys = along_y(x)
-        for i in range(vectors):
-            acc_ref[at, i * LANE : (i + 1) * LANE] = ys[i] + v_ref[:, i * LANE : (i + 1) * LANE] * x[i]
-        return 0
-
-    lax.fori_loop(0, rows // 8, eight, 0)
-    for g in range(groups):
+    x_all = rows_of(x_ref)
+    cache = {}
+    vector = lambda i: x_all[:, i * LANE : (i + 1) * LANE]
+    for g in range(length // GROUP):
         here = slice(g * GROUP, (g + 1) * GROUP)
-        x = flat_ref[:, here]
+        x = x_all[:, here]
         xh, xl = split(x)
         total = dot(jnp.concatenate([xh, xl, xh], axis=1), z_ref[...])
         total += dot(m_ref[...], stacked(jnp.concatenate([x, halo_ref[:, :, here].reshape(rows, GROUP)], axis=0)))
-        total += acc_ref[:, here]
-        out_ref[:, :, here] = total.reshape(count, planes, GROUP)
+        each = GROUP // LANE
+        total += jnp.concatenate([along_y(vector, length // LANE, g * each + i, cache) for i in range(each)], axis=1)
+        weighted = v_ref[:, here][None] * x.reshape(rows // 8, 8, GROUP)
+        out_ref[:, :, here] = (total + weighted.reshape(rows, GROUP)).reshape(count, planes, GROUP)
 
 
 def stencil(x, halo, odd, potential, block):
@@ -344,7 +338,6 @@
             grid=(count // block,),
             in_specs=[spec, spec, picked, fixed(z), fixed(v)],
             out_specs=spec,
-            scratch_shapes=[pltpu.VMEM((size, length), jnp.float32)] * 2,
         ),
         out_shape=jax.ShapeDtypeStruct(x.shape, jnp.float32),
         compiler_params=pltpu.CompilerParams(vmem_limit_bytes=VMEM),
@@ -452,18 +445,18 @@
     hb = [None] * nb
     hb[0] = stencil(mine, fast_mine, odd, potential, own)
     base = stencil(later, fast_later, odd, potential, min(32, count))
-    slots[1], slots[-1], hop, base, hb[0] = lax.optimization_barrier((slots[1], slots[-1], hop, base, hb[0]))
     for k in order[1:]:
         if slots[k] is None:
-            slots[k] = up(slots[k - 1]) if k <= middle else down(slots[k + 1])
+            slots[k] = up(after(slots[k - 1], base)) if k <= middle else down(after(slots[k + 1], base))
+    slots[1], slots[-1], hop, base, hb[0] = lax.optimization_barrier((slots[1], slots[-1], hop, base, hb[0]))
     far_later = lax.ppermute(hop, "space", hop_two)
     fast = {k: swap(slots[k]) for k in order[1:-1]}
     far_slow = {k: cross(slots[k]) for k in order[1:-1]}
     for k in order[1:-1]:
         hb[k] = stencil(slots[k], fast[k], odd, potential, own)
     known = gram([slots[k] for k in order[:-1]], after(later, *fast.values()))
-    slots[middle], known, slow_mine, *rest = lax.optimization_barrier(
-        (slots[middle], known, slow_mine, *[hb[k] for k in order[:-1]])
+    slots[middle], known, slow_mine, near_later, *rest = lax.optimization_barrier(
+        (slots[middle], known, slow_mine, near_later, *[hb[k] for k in order[:-1]])
     )
     for k, h in zip(order[:-1], rest):
         hb[k] = h

time: 215 us -> 213 us (level)
  Pallas kernels: 104 us -> 76.4 us
  local copies, waits for them, and re-layouts: 1.16 us -> 17.5 us
  waiting for transfers between devices: 50.2 us -> 58.4 us
    pallas_call x5, Pallas kernels: 56.1 us -> 35.8 us  [stencil(): pl.pallas_call(lambda odd_ref, *refs: stencil_kernel(*refs), grid_spec=pl...]
    unnamed x16 -> x52, local copies, waits for them, and re-layouts: 1.16 us -> 17.5 us
    ppermute x1, waiting for transfers between devices: 4.58 us -> 10.3 us  [local(): slow_mine = lax.ppermute(mine, 'space', near + far)]
    ppermute x2, waiting for transfers between devices: 28.2 us -> 31.5 us  [local(): up = lambda x: lax.ppermute(x, 'band', ring)]
    pallas_call x1, Pallas kernels: 17 us -> 14.6 us  [final(): pl.pallas_call(functools.partial(final_kernel, len(hb)), grid_spec=pltpu....]
    ppermute x5, waiting for transfers between devices: 5.48 us -> 3.32 us  [local(): swap = lambda x: lax.ppermute(x, 'space', fast_pairs)]
  transfers between devices with their start and end apart: 19 -> 19, of which waited for: 5 -> 5; matrix products, arithmetic and copies ran while one was open for 1% -> 0% of each run, Pallas kernels for 41% -> 30%
where the time goes in v2:
time: 213 us; the launch traced here: 209 us
  Pallas kernels  76.4 us (36%)
  waiting for transfers between devices  58.4 us (27%)
  starting transfers between devices  41.1 us (19%)
  local copies, waits for them, and re-layouts  17.5 us (8%)
  between operations  14.4 us (7%)
    pallas_call x5, Pallas kernels, stencil(): pl.pallas_call(lambda odd_ref, *refs: stencil_kernel(*refs), grid_spec=pl...  35.8 us
    ppermute x2, waiting for transfers between devices, local(): up = lambda x: lax.ppermute(x, 'band', ring)  31.5 us
    unnamed x52, local copies, waits for them, and re-layouts  17.5 us
    pallas_call x1, Pallas kernels, final(): pl.pallas_call(functools.partial(final_kernel, len(hb)), grid_spec=pltpu....  14.6 us
    ppermute x2, waiting for transfers between devices, local(): near_up = lambda x: lax.ppermute(x, both, near_ring)  13.2 us
    ppermute x2, starting transfers between devices, local(): near_up = lambda x: lax.ppermute(x, both, near_ring)  11.2 us
    ppermute x1, waiting for transfers between devices, local(): slow_mine = lax.ppermute(mine, 'space', near + far)  10.3 us
    pallas_call x1, Pallas kernels, gram(): pl.pallas_call(functools.partial(gram_kernel, len(slots)), grid=(length /...  9.02 us
  transfers between devices with their start and end apart: 19, of which 5 were waited for; matrix products, arithmetic and copies ran while one was open for 0% of the time, Pallas kernels for 30%

profile of v2, /device:TPU:6, one launch (start us, length us, event | category | flops | bytes accessed | tf_op | source)
XLA Modules:
  0.0 208.8 jit_solution(9467389052708958550)
XLA Ops:
  7.3 3.4 %collective-permute-start.2 = (f32[64,4,6144]{2,1,0:T(4,128)}, f32[64,4,6144]{2,1,0:T(4,128)}, u32[]{:S(2)}, u32[]{:S(2)}) collective-permute-start(f32[64,4,6144]{2,1,0:T(4,128)} %refs_4_.1), channel_id=1, source_target_pairs={{12,28},{16,0},{13,29},{17,1},{14,30},{18,2},{15,31},{19,3}} | collective-permute-start | bytes 18874376 | tf_op jit(solution)/shard_map/ppermute | solution.py:442
  10.6 3.3 %collective-permute-start.9 = (f32[64,4,6144]{2,1,0:T(4,128)}, f32[64,4,6144]{2,1,0:T(4,128)}, u32[]{:S(2)}, u32[]{:S(2)}) collective-permute-start(f32[64,4,6144]{2,1,0:T(4,128)} %refs_4_.1), channel_id=1, source_target_pairs={{4,8},{20,24},{8,4},{24,20},{5,9},{21,25},{9,5},{25,21},{6,10},{22... | collective-permute-start | bytes 18874376 | tf_op jit(solution)/shard_map/ppermute | solution.py:443
  13.9 2.7 %collective-permute-start.1 = (f32[16,4,6144]{2,1,0:T(4,128)}, f32[16,4,6144]{2,1,0:T(4,128)}, u32[]{:S(2)}, u32[]{:S(2)}) collective-permute-start(f32[16,4,6144]{2,1,0:T(4,128)} %bitcast.12), channel_id=1, source_target_pairs={{0,1},{1,2},{2,3},{3,0},{4,5},{5,6},{6,7},{7,4},{8,9},{9,10},{10,1... | collective-permute-start | bytes 4718600 | tf_op jit(solution)/shard_map/ppermute | solution.py:431
  16.6 3.3 %collective-permute-done.4.refs_1_ = f32[16,4,6144]{2,1,0:T(4,128)S(1)} collective-permute-done((f32[16,4,6144]{2,1,0:T(4,128)}, f32[16,4,6144]{2,1,0:T(4,128)S(1)}, u32[]{:S(2)}, u32[]{:S(2)}) %collective-permute-start.4) | collective-permute-done | bytes 1572896 | tf_op jit(solution)/shard_map/ppermute | solution.py:432
  21.0 3.6 %collective-permute-start = (f32[16,4,6144]{2,1,0:T(4,128)}, f32[16,4,6144]{2,1,0:T(4,128)}, u32[]{:S(2)}, u32[]{:S(2)}) collective-permute-start(f32[16,4,6144]{2,1,0:T(4,128)} %bitcast.13), channel_id=1, source_target_pairs={{1,0},{2,1},{3,2},{0,3},{5,4},{6,5},{7,6},{4,7},{9,8},{10,9},{11,1... | collective-permute-start | bytes 4718600 | tf_op jit(solution)/shard_map/ppermute | solution.py:430
  25.7 1.4 copy-done.9
  27.1 1.4 copy-done.12
  30.5 3.9 %stencil.6.refs_0_ = f32[16,4,6144]{2,1,0:T(4,128)S(1)} custom-call(s32[1]{0:T(128)} %bitcast.1.odd_ref, f32[16,4,6144]{2,1,0:T(4,128)S(1)} %bitcast.14, f32[16,4,6144]{2,1,0:T(4,128)S(1)} %copy-done.12, bf16[2,64,384]{2,1,0:T(8,128)(2,1)S(1)} %copy-done.18, bf16[1152,384]{1,0:T(8,128)(2,1)S(1)} %copy-done.14, f32[8,6144]{1,0:T(8,128)S(1)} %pad_maximum_fusion.refs_4_), custom_call_target="tpu_custom_call" | custom-call | flops 1600000000 | bytes 4718592 | tf_op jit(solution)/shard_map/stencil/pallas_call | solution.py:334
  34.5 2.8 %copy-done.8 = f32[64,4,6144]{2,1,0:T(4,128)S(1)} copy-done((f32[64,4,6144]{2,1,0:T(4,128)S(1)}, f32[64,4,6144]{2,1,0:T(4,128)}, u32[]{:S(2)}) %copy-start.8) | copy-done | bytes 6291480
  37.3 15.1 %stencil.5.base_ref = f32[64,4,6144]{2,1,0:T(4,128)S(1)} custom-call(s32[1]{0:T(128)} %bitcast.1.odd_ref, f32[64,4,6144]{2,1,0:T(4,128)S(1)} %copy-done.8, f32[64,4,6144]{2,1,0:T(4,128)} %collective-permute-done.3.refs_1_, bf16[2,128,768]{2,1,0:T(8,128)(2,1)S(1)} %copy-done.17, bf16[1152,384]{1,0:T(8,128)(2,1)S(1)} %copy-done.15, ...), custom_call_target="tpu_custom_call" | custom-call | flops 6400000000 | bytes 18874368 | tf_op jit(solution)/shard_map/stencil/pallas_call | solution.py:334
  52.5 2.7 %copy-done = f32[64,4,6144]{2,1,0:T(4,128)} copy-done((f32[64,4,6144]{2,1,0:T(4,128)}, f32[64,4,6144]{2,1,0:T(4,128)S(1)}, u32[]{:S(2)}) %copy-start) | copy-done | bytes 6291480
  55.2 31.5 %collective-permute-done.refs_1_.refs_0_ = f32[16,4,6144]{2,1,0:T(4,128)} collective-permute-done((f32[16,4,6144]{2,1,0:T(4,128)}, f32[16,4,6144]{2,1,0:T(4,128)}, u32[]{:S(2)}, u32[]{:S(2)}) %collective-permute-start) | collective-permute-done | bytes 1572896 | tf_op jit(solution)/shard_map/ppermute | solution.py:430
  86.7 3.3 %collective-permute-start.10 = (f32[64,4,6144]{2,1,0:T(4,128)}, f32[64,4,6144]{2,1,0:T(4,128)}, u32[]{:S(2)}, u32[]{:S(2)}) collective-permute-start(f32[64,4,6144]{2,1,0:T(4,128)} %collective-permute-done.2), channel_id=1, source_target_pairs={{28,16},{0,12},{29,17},{1,13},{30,18},{2,14},{31,19},{3,15}} | collective-permute-start | bytes 18874376 | tf_op jit(solution)/shard_map/ppermute | solution.py:452
  90.0 2.3 %collective-permute-start.7 = (f32[16,4,6144]{2,1,0:T(4,128)}, f32[16,4,6144]{2,1,0:T(4,128)S(1)}, u32[]{:S(2)}, u32[]{:S(2)}) collective-permute-start(f32[16,4,6144]{2,1,0:T(4,128)} %collective-permute-done.1.refs_2_.refs_0_), channel_id=1, source_target_pairs={{0,4},{4,0},{8,12},{12,8},{16,20},{20,16},{24,28},{28,24},{1,5},{5... | collective-permute-start | bytes 4718600 | tf_op jit(solution)/shard_map/ppermute | solution.py:432
  92.3 1.9 collective-permute-start.8
  94.2 1.8 collective-permute-start.5
  96.0 2.0 collective-permute-start.15
  98.0 5.4 %stencil.7.refs_1_ = f32[16,4,6144]{2,1,0:T(4,128)S(1)} custom-call(s32[1]{0:T(128)} %bitcast.1.odd_ref, f32[16,4,6144]{2,1,0:T(4,128)} %collective-permute-done.refs_1_.refs_0_, f32[16,4,6144]{2,1,0:T(4,128)S(1)} %collective-permute-done.6.refs_1_, bf16[2,64,384]{2,1,0:T(8,128)(2,1)S(1)} %copy-done.19, bf16[1152,384]{1,0:T(8,128)(2,1)S(1)} %copy-done.15, ...), custom_call_target="tpu_custom_call" | custom-call | flops 1600000000 | bytes 4718592 | tf_op jit(solution)/shard_map/stencil/pallas_call | solution.py:334
  104.5 5.5 %stencil.8.refs_2_ = f32[16,4,6144]{2,1,0:T(4,128)S(1)} custom-call(s32[1]{0:T(128)} %bitcast.1.odd_ref, f32[16,4,6144]{2,1,0:T(4,128)} %collective-permute-done.1.refs_2_.refs_0_, f32[16,4,6144]{2,1,0:T(4,128)S(1)} %collective-permute-done.7.refs_1_, bf16[2,64,384]{2,1,0:T(8,128)(2,1)S(1)} %copy-done.19, bf16[1152,384]{1,0:T(8,128)(2,1)S(1)} %copy-done.15, ...), custom_call_target="tpu_custom_call" | custom-call | flops 1600000000 | bytes 4718592 | tf_op jit(solution)/shard_map/stencil/pallas_call | solution.py:334
  111.2 9.0 %gram.1.refs_5_ = f32[48,128]{1,0:T(8,128)S(1)} custom-call(f32[16,4,6144]{2,1,0:T(4,128)S(1)} %bitcast.16, f32[16,4,6144]{2,1,0:T(4,128)} %collective-permute-done.refs_1_.refs_0_, f32[16,4,6144]{2,1,0:T(4,128)} %collective-permute-done.1.refs_2_.refs_0_, f32[64,4,6144]{2,1,0:T(4,128)S(1)} %copy-done.8), custom_call_target="tpu_custom_call" | custom-call | flops 8000000000 | bytes 11010048 | tf_op jit(solution)/shard_map/gram/pallas_call | solution.py:132
  120.2 10.3 %collective-permute-done.8.refs_4_ = f32[16,4,6144]{2,1,0:T(4,128)S(1)} collective-permute-done((f32[16,4,6144]{2,1,0:T(4,128)S(1)}, f32[16,4,6144]{2,1,0:T(4,128)S(1)}, u32[]{:S(2)}, u32[]{:S(2)}) %collective-permute-start.8) | collective-permute-done | bytes 1572896 | tf_op jit(solution)/shard_map/ppermute | solution.py:444
  130.6 4.5 %collective-permute-start.12 = (f32[16,4,6144]{2,1,0:T(4,128)S(1)}, f32[16,4,6144]{2,1,0:T(4,128)}, u32[]{:S(2)}, u32[]{:S(2)}) collective-permute-start(f32[16,4,6144]{2,1,0:T(4,128)S(1)} %collective-permute-done.8.refs_4_), channel_id=1, source_target_pairs={{5,4},{6,5},{7,6},{4,7},{21,20},{22,21},{23,22},{20,23},{9,8},{10,... | collective-permute-start | bytes 4718600 | tf_op jit(solution)/shard_map/ppermute | solution.py:434
  135.2 9.0 %gram_last.1 = f32[256,128]{1,0:T(8,128)} custom-call(f32[16,4,6144]{2,1,0:T(4,128)S(1)} %bitcast.17, f32[16,4,6144]{2,1,0:T(4,128)} %collective-permute-done.refs_1_.refs_0_, f32[16,4,6144]{2,1,0:T(4,128)} %collective-permute-done.1.refs_2_.refs_0_, f32[16,4,6144]{2,1,0:T(4,128)} %collective-permute-done.5.refs_0_.refs_3_, f32[64,4,6144]{2,1,0:T(4,128)S(1)} %bitcast.10, ...), custom_call_target="tpu_custom_call" | custom-call | flops 4000000000 | bytes 12582912 | tf_op jit(solution)/shard_map/gram_last/pallas_call | solution.py:186
  144.2 1.9 collective-permute-start.16
  146.1 1.9 collective-permute-start.13
  148.1 5.0 %collective-permute-done.12.refs_5_ = f32[16,4,6144]{2,1,0:T(4,128)} collective-permute-done((f32[16,4,6144]{2,1,0:T(4,128)S(1)}, f32[16,4,6144]{2,1,0:T(4,128)}, u32[]{:S(2)}, u32[]{:S(2)}) %collective-permute-start.12) | collective-permute-done | bytes 1572896 | tf_op jit(solution)/shard_map/ppermute | solution.py:434
  153.1 1.8 collective-permute-start.17
  154.9 6.6 %collective-permute-start.14 = (f32[16,4,6144]{2,1,0:T(4,128)}, f32[16,4,6144]{2,1,0:T(4,128)}, u32[]{:S(2)}, u32[]{:S(2)}) collective-permute-start(f32[16,4,6144]{2,1,0:T(4,128)} %collective-permute-done.12.refs_5_), channel_id=1, source_target_pairs={{5,4},{6,5},{7,6},{4,7},{21,20},{22,21},{23,22},{20,23},{9,8},{10,... | collective-permute-start | bytes 4718600 | tf_op jit(solution)/shard_map/ppermute | solution.py:434
  162.8 5.9 %stencil.9.refs_3_ = f32[16,4,6144]{2,1,0:T(4,128)S(1)} custom-call(s32[1]{0:T(128)} %bitcast.1.odd_ref, f32[16,4,6144]{2,1,0:T(4,128)} %collective-permute-done.5.refs_0_.refs_3_, f32[16,4,6144]{2,1,0:T(4,128)} %collective-permute-done.11.refs_1_, bf16[2,64,384]{2,1,0:T(8,128)(2,1)S(1)} %copy-done.19, bf16[1152,384]{1,0:T(8,128)(2,1)S(1)} %copy-done.16, ...), custom_call_target="tpu_custom_call" | custom-call | flops 1600000000 | bytes 4718592 | tf_op jit(solution)/shard_map/stencil/pallas_call | solution.py:334
  171.2 7.9 %mix.1.refs_12_ = bf16[320,1536]{1,0:T(8,128)(2,1)S(1)} custom-call(s32[1]{0:T(128)} %bitcast.4.band_ref, f32[4,4]{1,0:T(4,128)S(1)} %select_select_fusion.slow_ref, f32[8,256,128]{2,1,0:T(8,128)S(1)} %bitcast.18), custom_call_target="tpu_custom_call" | custom-call | flops 10000000000 | bytes 1048576 | tf_op jit(solution)/shard_map/mix/pallas_call | solution.py:269
  179.1 8.2 %collective-permute-done.14.refs_7_ = f32[16,4,6144]{2,1,0:T(4,128)} collective-permute-done((f32[16,4,6144]{2,1,0:T(4,128)}, f32[16,4,6144]{2,1,0:T(4,128)}, u32[]{:S(2)}, u32[]{:S(2)}) %collective-permute-start.14) | collective-permute-done | bytes 1572896 | tf_op jit(solution)/shard_map/ppermute | solution.py:434
  187.4 14.6 %final.1 = (f32[64,4,6144]{2,1,0:T(4,128)}, f32[16,4,6144]{2,1,0:T(4,128)}) custom-call(s32[1]{0:T(128)S(6)} %select_n.41.kind_ref, s32[1]{0:T(128)} %bitcast.2.far_ref, f32[64,4,6144]{2,1,0:T(4,128)S(1)} %bitcast.8, f32[64,4,6144]{2,1,0:T(4,128)} %collective-permute-done.9.near_later, f32[64,4,6144]{2,1,0:T(4,128)} %collective-permute-done.10.far_later, ...), custom_call_target="tpu_custom_call" | custom-call | flops 8000000000 | bytes 37748736 | tf_op jit(solution)/shard_map/final/pallas_call | solution.py:375
  (72 shorter events, 10.5 us)
Async XLA Ops:
  7.2 162.6 %all-gather.3.cloned.1.call-start = ((), (), s32[]{:S(2)}) async-start(), calls=%async_computation | async-start | bytes 1179648 | tf_op jit(solution)/shard_map/all_gather | solution.py:468
  7.2 27.3 %collective-permute-start.3 = (f32[64,4,6144]{2,1,0:T(4,128)}, f32[64,4,6144]{2,1,0:T(4,128)}, u32[]{:S(2)}, u32[]{:S(2)}) collective-permute-start(f32[64,4,6144]{2,1,0:T(4,128)} %refs_4_.1), channel_id=1, source_target_pairs={{0,4},{4,0},{8,12},{12,8},{16,20},{20,16},{24,28},{28,24},{1,5},{5... | collective-permute-start | bytes 18874376 | tf_op jit(solution)/shard_map/ppermute | solution.py:432
  7.3 79.4 %collective-permute-start.2 = (f32[64,4,6144]{2,1,0:T(4,128)}, f32[64,4,6144]{2,1,0:T(4,128)}, u32[]{:S(2)}, u32[]{:S(2)}) collective-permute-start(f32[64,4,6144]{2,1,0:T(4,128)} %refs_4_.1), channel_id=1, source_target_pairs={{12,28},{16,0},{13,29},{17,1},{14,30},{18,2},{15,31},{19,3}} | collective-permute-start | bytes 18874376 | tf_op jit(solution)/shard_map/ppermute | solution.py:442
  10.6 9.2 %collective-permute-start.4 = (f32[16,4,6144]{2,1,0:T(4,128)}, f32[16,4,6144]{2,1,0:T(4,128)S(1)}, u32[]{:S(2)}, u32[]{:S(2)}) collective-permute-start(f32[16,4,6144]{2,1,0:T(4,128)} %bitcast.11), channel_id=1, source_target_pairs={{0,4},{4,0},{8,12},{12,8},{16,20},{20,16},{24,28},{28,24},{1,5},{5... | collective-permute-start | bytes 4718600 | tf_op jit(solution)/shard_map/ppermute | solution.py:432
  10.6 119.9 %collective-permute-start.9 = (f32[64,4,6144]{2,1,0:T(4,128)}, f32[64,4,6144]{2,1,0:T(4,128)}, u32[]{:S(2)}, u32[]{:S(2)}) collective-permute-start(f32[64,4,6144]{2,1,0:T(4,128)} %refs_4_.1), channel_id=1, source_target_pairs={{4,8},{20,24},{8,4},{24,20},{5,9},{21,25},{9,5},{25,21},{6,10},{22... | collective-permute-start | bytes 18874376 | tf_op jit(solution)/shard_map/ppermute | solution.py:443
  13.9 41.2 %collective-permute-start.1 = (f32[16,4,6144]{2,1,0:T(4,128)}, f32[16,4,6144]{2,1,0:T(4,128)}, u32[]{:S(2)}, u32[]{:S(2)}) collective-permute-start(f32[16,4,6144]{2,1,0:T(4,128)} %bitcast.12), channel_id=1, source_target_pairs={{0,1},{1,2},{2,3},{3,0},{4,5},{5,6},{6,7},{7,4},{8,9},{9,10},{10,1... | collective-permute-start | bytes 4718600 | tf_op jit(solution)/shard_map/ppermute | solution.py:431
  21.0 65.6 %collective-permute-start = (f32[16,4,6144]{2,1,0:T(4,128)}, f32[16,4,6144]{2,1,0:T(4,128)}, u32[]{:S(2)}, u32[]{:S(2)}) collective-permute-start(f32[16,4,6144]{2,1,0:T(4,128)} %bitcast.13), channel_id=1, source_target_pairs={{1,0},{2,1},{3,2},{0,3},{5,4},{6,5},{7,6},{4,7},{9,8},{10,9},{11,1... | collective-permute-start | bytes 4718600 | tf_op jit(solution)/shard_map/ppermute | solution.py:430
  30.5 4.0 %copy-start.17 = (bf16[2,128,768]{2,1,0:T(8,128)(2,1)S(1)}, bf16[2,128,768]{2,1,0:T(8,128)(2,1)}, u32[]{:S(2)}) copy-start(bf16[2,128,768]{2,1,0:T(8,128)(2,1)} %constant.63.clone.refs_2_) | copy-start | bytes 1179652
  37.3 54.9 %copy-start.10 = (f32[2,8,4,6144]{3,2,1,0:T(4,128)S(1)}, f32[2,8,4,6144]{3,2,1,0:T(4,128)}, u32[]{:S(2)}) copy-start(f32[2,8,4,6144]{3,2,1,0:T(4,128)} %param.21) | copy-start | bytes 4718596
  37.3 60.6 %copy-start.19 = (bf16[2,64,384]{2,1,0:T(8,128)(2,1)S(1)}, bf16[2,64,384]{2,1,0:T(8,128)(2,1)}, u32[]{:S(2)}) copy-start(bf16[2,64,384]{2,1,0:T(8,128)(2,1)} %constant.60.clone.refs_2_) | copy-start | bytes 294916
  86.7 7.5 %collective-permute-start.6 = (f32[16,4,6144]{2,1,0:T(4,128)}, f32[16,4,6144]{2,1,0:T(4,128)S(1)}, u32[]{:S(2)}, u32[]{:S(2)}) collective-permute-start(f32[16,4,6144]{2,1,0:T(4,128)} %collective-permute-done.refs_1_.refs_0_), channel_id=1, source_target_pairs={{0,4},{4,0},{8,12},{12,8},{16,20},{20,16},{24,28},{28,24},{1,5},{5... | collective-permute-start | bytes 4718600 | tf_op jit(solution)/shard_map/ppermute | solution.py:432
  86.7 100.6 %collective-permute-start.10 = (f32[64,4,6144]{2,1,0:T(4,128)}, f32[64,4,6144]{2,1,0:T(4,128)}, u32[]{:S(2)}, u32[]{:S(2)}) collective-permute-start(f32[64,4,6144]{2,1,0:T(4,128)} %collective-permute-done.2), channel_id=1, source_target_pairs={{28,16},{0,12},{29,17},{1,13},{30,18},{2,14},{31,19},{3,15}} | collective-permute-start | bytes 18874376 | tf_op jit(solution)/shard_map/ppermute | solution.py:452
  90.0 6.0 %collective-permute-start.7 = (f32[16,4,6144]{2,1,0:T(4,128)}, f32[16,4,6144]{2,1,0:T(4,128)S(1)}, u32[]{:S(2)}, u32[]{:S(2)}) collective-permute-start(f32[16,4,6144]{2,1,0:T(4,128)} %collective-permute-done.1.refs_2_.refs_0_), channel_id=1, source_target_pairs={{0,4},{4,0},{8,12},{12,8},{16,20},{20,16},{24,28},{28,24},{1,5},{5... | collective-permute-start | bytes 4718600 | tf_op jit(solution)/shard_map/ppermute | solution.py:432
  92.3 38.3 %collective-permute-start.8 = (f32[16,4,6144]{2,1,0:T(4,128)S(1)}, f32[16,4,6144]{2,1,0:T(4,128)S(1)}, u32[]{:S(2)}, u32[]{:S(2)}) collective-permute-start(f32[16,4,6144]{2,1,0:T(4,128)S(1)} %bitcast.15), channel_id=1, source_target_pairs={{4,8},{20,24},{8,4},{24,20},{12,16},{16,12},{5,9},{21,25},{9,5},{2... | collective-permute-start | bytes 4718600 | tf_op jit(solution)/shard_map/ppermute | solution.py:444
  94.2 36.4 %collective-permute-start.5 = (f32[16,4,6144]{2,1,0:T(4,128)}, f32[16,4,6144]{2,1,0:T(4,128)}, u32[]{:S(2)}, u32[]{:S(2)}) collective-permute-start(f32[16,4,6144]{2,1,0:T(4,128)} %collective-permute-done.refs_1_.refs_0_), channel_id=1, source_target_pairs={{1,0},{2,1},{3,2},{0,3},{5,4},{6,5},{7,6},{4,7},{9,8},{10,9},{11,1... | collective-permute-start | bytes 4718600 | tf_op jit(solution)/shard_map/ppermute | solution.py:430
  96.0 50.2 %collective-permute-start.15 = (f32[16,4,6144]{2,1,0:T(4,128)}, f32[16,4,6144]{2,1,0:T(4,128)}, u32[]{:S(2)}, u32[]{:S(2)}) collective-permute-start(f32[16,4,6144]{2,1,0:T(4,128)} %collective-permute-done.refs_1_.refs_0_), channel_id=1, source_target_pairs={{12,16},{16,12},{13,17},{17,13},{14,18},{18,14},{15,19},{19,15}} | collective-permute-start | bytes 4718600 | tf_op jit(solution)/shard_map/ppermute | solution.py:436
  104.5 30.7 %slice-start.2 = ((s8[6291456]{0:T(1024)(128)(4,1)}), s8[4194304]{0:T(1024)(128)(4,1)S(1)}, s32[]{:S(2)}) async-start(s8[6291456]{0:T(1024)(128)(4,1)} %bitcast.9), calls=%async_computation.3 | async-start | bytes 8388608
  111.2 24.0 %slice-start.3 = ((s8[6291456]{0:T(1024)(128)(4,1)}), s8[2097152]{0:T(1024)(128)(4,1)S(1)}, s32[]{:S(2)}) async-start(s8[6291456]{0:T(1024)(128)(4,1)} %bitcast.9), calls=%async_computation.4 | async-start | bytes 4194304
  120.2 41.4 %copy-start.20 = (f32[4,4]{1,0:T(4,128)S(1)}, f32[4,4]{1,0:T(4,128)}, u32[]{:S(2)}) copy-start(f32[4,4]{1,0:T(4,128)} %constant.59.clone) | copy-start | bytes 196
  120.2 41.4 %copy-start.21 = (f32[4,4]{1,0:T(4,128)S(1)}, f32[4,4]{1,0:T(4,128)}, u32[]{:S(2)}) copy-start(f32[4,4]{1,0:T(4,128)} %constant.58.clone) | copy-start | bytes 196
  130.6 22.5 %collective-permute-start.12 = (f32[16,4,6144]{2,1,0:T(4,128)S(1)}, f32[16,4,6144]{2,1,0:T(4,128)}, u32[]{:S(2)}, u32[]{:S(2)}) collective-permute-start(f32[16,4,6144]{2,1,0:T(4,128)S(1)} %collective-permute-done.8.refs_4_), channel_id=1, source_target_pairs={{5,4},{6,5},{7,6},{4,7},{21,20},{22,21},{23,22},{20,23},{9,8},{10,... | collective-permute-start | bytes 4718600 | tf_op jit(solution)/shard_map/ppermute | solution.py:434
  135.1 19.8 %collective-permute-start.11 = (f32[16,4,6144]{2,1,0:T(4,128)}, f32[16,4,6144]{2,1,0:T(4,128)}, u32[]{:S(2)}, u32[]{:S(2)}) collective-permute-start(f32[16,4,6144]{2,1,0:T(4,128)} %collective-permute-done.5.refs_0_.refs_3_), channel_id=1, source_target_pairs={{0,4},{4,0},{8,12},{12,8},{16,20},{20,16},{24,28},{28,24},{1,5},{5... | collective-permute-start | bytes 4718600 | tf_op jit(solution)/shard_map/ppermute | solution.py:432
  144.2 34.9 %collective-permute-start.16 = (f32[16,4,6144]{2,1,0:T(4,128)}, f32[16,4,6144]{2,1,0:T(4,128)}, u32[]{:S(2)}, u32[]{:S(2)}) collective-permute-start(f32[16,4,6144]{2,1,0:T(4,128)} %collective-permute-done.1.refs_2_.refs_0_), channel_id=1, source_target_pairs={{12,16},{16,12},{13,17},{17,13},{14,18},{18,14},{15,19},{19,15}} | collective-permute-start | bytes 4718600 | tf_op jit(solution)/shard_map/ppermute | solution.py:436
  146.1 33.0 %collective-permute-start.13 = (f32[16,4,6144]{2,1,0:T(4,128)S(1)}, f32[16,4,6144]{2,1,0:T(4,128)}, u32[]{:S(2)}, u32[]{:S(2)}) collective-permute-start(f32[16,4,6144]{2,1,0:T(4,128)S(1)} %collective-permute-done.8.refs_4_), channel_id=1, source_target_pairs={{4,5},{5,6},{6,7},{7,4},{20,21},{21,22},{22,23},{23,20},{8,9},{9,1... | collective-permute-start | bytes 4718600 | tf_op jit(solution)/shard_map/ppermute | solution.py:435
  153.1 26.0 %collective-permute-start.17 = (f32[16,4,6144]{2,1,0:T(4,128)}, f32[16,4,6144]{2,1,0:T(4,128)}, u32[]{:S(2)}, u32[]{:S(2)}) collective-permute-start(f32[16,4,6144]{2,1,0:T(4,128)} %collective-permute-done.5.refs_0_.refs_3_), channel_id=1, source_target_pairs={{12,16},{16,12},{13,17},{17,13},{14,18},{18,14},{15,19},{19,15}} | collective-permute-start | bytes 4718600 | tf_op jit(solution)/shard_map/ppermute | solution.py:436
  154.9 32.4 %collective-permute-start.14 = (f32[16,4,6144]{2,1,0:T(4,128)}, f32[16,4,6144]{2,1,0:T(4,128)}, u32[]{:S(2)}, u32[]{:S(2)}) collective-permute-start(f32[16,4,6144]{2,1,0:T(4,128)} %collective-permute-done.12.refs_5_), channel_id=1, source_target_pairs={{5,4},{6,5},{7,6},{4,7},{21,20},{22,21},{23,22},{20,23},{9,8},{10,... | collective-permute-start | bytes 4718600 | tf_op jit(solution)/shard_map/ppermute | solution.py:434
  169.8 17.6 %slice-start = ((s8[6291456]{0:T(1024)(128)(4,1)}), s8[4194304]{0:T(1024)(128)(4,1)S(1)}, s32[]{:S(2)}) async-start(s8[6291456]{0:T(1024)(128)(4,1)} %bitcast.7), calls=%async_computation.1 | async-start | bytes 8388608
  171.2 16.2 %slice-start.1 = ((s8[6291456]{0:T(1024)(128)(4,1)}), s8[2097152]{0:T(1024)(128)(4,1)S(1)}, s32[]{:S(2)}) async-start(s8[6291456]{0:T(1024)(128)(4,1)} %bitcast.7), calls=%async_computation.2 | async-start | bytes 4194304
  171.2 16.2 %copy-start.2 = (f32[16,4,6144]{2,1,0:T(4,128)S(1)}, f32[16,4,6144]{2,1,0:T(4,128)}, u32[]{:S(2)}) copy-start(f32[16,4,6144]{2,1,0:T(4,128)} %copy-done.1) | copy-start | bytes 4718596
  171.2 16.2 %copy-start.4 = (f32[16,4,6144]{2,1,0:T(4,128)S(1)}, f32[16,4,6144]{2,1,0:T(4,128)}, u32[]{:S(2)}) copy-start(f32[16,4,6144]{2,1,0:T(4,128)} %copy-done.3) | copy-start | bytes 4718596
  171.2 16.2 %copy-start.6 = (f32[16,4,6144]{2,1,0:T(4,128)S(1)}, f32[16,4,6144]{2,1,0:T(4,128)}, u32[]{:S(2)}) copy-start(f32[16,4,6144]{2,1,0:T(4,128)} %copy-done.5) | copy-start | bytes 4718596
  171.2 16.2 %copy-start.7 = (bf16[3,256,768]{2,1,0:T(8,128)(2,1)S(1)}, bf16[3,256,768]{2,1,0:T(8,128)(2,1)}, u32[]{:S(2)}) copy-start(bf16[3,256,768]{2,1,0:T(8,128)(2,1)} %constant.64.clone.refs_11_) | copy-start | bytes 3538948
  (13 other events, 21.5 us)
Sparse Core Ops, SparseCore 0:
  144.4 24.1 all-gather.2
